TPU v7x, 32 devices: a whole 2x2x4 slice. The times are simulated.
32 devices in a mesh: dp: 8 (over y, x, core), ctx: 4 (over z).
Axes of the slice: x: 2, y: 2, z: 4, core: 2. Of those that a mesh axis runs over, the one named last changes fastest.
Arguments:
- tokens: bfloat16 [2, 8, 1024, 576], P(None, 'dp', 'ctx'), may hold values from -6 to 6
- span_order: int32 [2, 8, 4], P(None, 'dp'), may hold values from 0 to 3, each once within a row
- cotangent: bfloat16 [2, 8, 1024, 576], P(None, 'dp', 'ctx'), may hold values from -6 to 6
- query_weight: bfloat16 [576, 576], P('dp', 'ctx'), may hold values from -0.25 to 0.25
- key_weight: bfloat16 [576, 192], P('dp', 'ctx'), may hold values from -0.25 to 0.25
- value_weight: bfloat16 [576, 192], P('dp', 'ctx'), may hold values from -0.25 to 0.25
- output_weight: bfloat16 [576, 576], P('dp', 'ctx'), may hold values from -1.5 to 1.5
- gate_weight: bfloat16 [576, 1536], P('dp', 'ctx'), may hold values from -0.25 to 0.25
- up_weight: bfloat16 [576, 1536], P('dp', 'ctx'), may hold values from -0.25 to 0.25
- down_weight: bfloat16 [1536, 576], P('dp', 'ctx'), may hold values from -0.15625 to 0.15625
- attention_gain: bfloat16 [576], P('dp'), may hold values from 0.25 to 1.75
- feedforward_gain: bfloat16 [576], P('dp'), may hold values from 0.25 to 1.75
Outputs:
- layer_output: bfloat16 [2, 8, 1024, 576], P(None, 'dp', 'ctx')
- input_grad: float32 [2, 8, 1024, 576], P(None, 'dp', 'ctx')
- query_grad: float32 [576, 576], P('dp', 'ctx')
- key_grad: float32 [576, 192], P('dp', 'ctx')
- value_grad: float32 [576, 192], P('dp', 'ctx')
- output_grad: float32 [576, 576], P('dp', 'ctx')
- gate_grad: float32 [576, 1536], P('dp', 'ctx')
- up_grad: float32 [576, 1536], P('dp', 'ctx')
- down_grad: float32 [1536, 576], P('dp', 'ctx')
- attention_gain_grad: float32 [576], P('dp')
- feedforward_gain_grad: float32 [576], P('dp')
Inputs may be any that keep to these rules, and one draw needn't show every extreme that they name: `span_order`: for every micro-batch and sequence the 4 entries are the span numbers 0 to 3, each once.
All inputs are finite; a program needn't handle non-finite values.
Results may differ from a plain program's by a relative error of at most 0.02.
Values may be sent and summed in bfloat16 or wider, within the bound.
A program may use at most 128 MiB of HBM per device.

v0:
```python
import jax
import jax.numpy as jnp
from jax import lax
from jax.sharding import PartitionSpec as P

HEADS = 9
KV_HEADS = 3
HEAD_DIM = 64


EPSILON = 1e-05
NEG_FILL = -1e30


def rotate(values, cos_table, sin_table):
    half_dim = values.shape[-1] // 2
    lower_half = values[..., :half_dim]
    upper_half = values[..., half_dim:]
    return jnp.concatenate(
        [
            lower_half * cos_table - upper_half * sin_table,
            upper_half * cos_table + lower_half * sin_table,
        ],
        axis=-1,
    )


def unrotate(values, cos_table, sin_table):
    half_dim = values.shape[-1] // 2
    lower_half = values[..., :half_dim]
    upper_half = values[..., half_dim:]
    return jnp.concatenate(
        [
            lower_half * cos_table + upper_half * sin_table,
            upper_half * cos_table - lower_half * sin_table,
        ],
        axis=-1,
    )


def angle_tables(position):
    inverse_freq = 1.0 / 10000.0 ** (jnp.arange(0, HEAD_DIM, 2).astype(jnp.float32) / HEAD_DIM)
    angle_table = position.astype(jnp.float32)[..., None] * inverse_freq
    return (jnp.cos(angle_table)[:, :, None, :], jnp.sin(angle_table)[:, :, None, :])


def rows_product(left_mat, right_mat):
    return lax.dot_general(
        left_mat, right_mat, (((0,), (0,)), ((), ())), preferred_element_type=jnp.float32
    )


def transposed_product(left_mat, right_mat):
    return lax.dot_general(
        left_mat, right_mat, (((1,), (1,)), ((), ())), preferred_element_type=jnp.float32
    )


def gather_weights(
    query_weight,
    key_weight,
    value_weight,
    output_weight,
    gate_weight,
    up_weight,
    down_weight,
    attention_gain,
    feedforward_gain,
):
    wide_mats = (
        lax.all_gather(query_weight, "ctx", axis=1, tiled=True),
        lax.all_gather(key_weight, "ctx", axis=1, tiled=True),
        lax.all_gather(value_weight, "ctx", axis=1, tiled=True),
        lax.all_gather(output_weight, "ctx", axis=1, tiled=True),
        lax.all_gather(gate_weight, "ctx", axis=1, tiled=True),
        lax.all_gather(up_weight, "ctx", axis=1, tiled=True),
        lax.all_gather(down_weight, "ctx", axis=1, tiled=True),
    )
    whole_set = (
        lax.all_gather(wide_mats[0], "dp", axis=0, tiled=True),
        lax.all_gather(wide_mats[1], "dp", axis=0, tiled=True),
        lax.all_gather(wide_mats[2], "dp", axis=0, tiled=True),
        lax.all_gather(wide_mats[3], "dp", axis=0, tiled=True),
        lax.all_gather(wide_mats[4], "dp", axis=0, tiled=True),
        lax.all_gather(wide_mats[5], "dp", axis=0, tiled=True),
        lax.all_gather(wide_mats[6], "dp", axis=0, tiled=True),
        lax.all_gather(attention_gain, "dp", axis=0, tiled=True),
        lax.all_gather(feedforward_gain, "dp", axis=0, tiled=True),
    )
    return whole_set


def masked_scores(query_rot, key_all, query_pos, key_pos):
    seq_count, span_len = (query_rot.shape[0], query_rot.shape[1])
    group_size = HEADS // KV_HEADS
    query_groups = query_rot.reshape(seq_count, span_len, KV_HEADS, group_size, HEAD_DIM)
    key_heads = key_all.reshape(seq_count, key_all.shape[1], KV_HEADS, HEAD_DIM)
    raw_scores = jnp.einsum(
        "sqhgd,skhd->shgqk", query_groups, key_heads, preferred_element_type=jnp.float32
    )
    allowed = (key_pos[:, None, :] <= query_pos[:, :, None])[:, None, None, :, :]
    return jnp.where(allowed, raw_scores * HEAD_DIM ** (-0.5), NEG_FILL)


def forward_pass(micro_tokens, micro_order, whole_set, ctx_index):
    query_mat, key_mat, value_mat, output_mat, gate_mat, up_mat, down_mat = whole_set[:7]
    attn_gain = whole_set[7].astype(jnp.float32)
    ffn_gain = whole_set[8].astype(jnp.float32)
    seq_count, span_len, model_width = micro_tokens.shape
    row_count = seq_count * span_len
    ctx_parts = micro_order.shape[1]
    sequence = micro_tokens.astype(jnp.float32).reshape(row_count, model_width)
    inverse_one = lax.rsqrt(jnp.mean(sequence * sequence, axis=-1, keepdims=True) + EPSILON)
    norm_one = sequence * inverse_one
    normed = (norm_one * attn_gain).astype(jnp.bfloat16)
    query_pre = jnp.dot(normed, query_mat, preferred_element_type=jnp.float32)
    key_pre = jnp.dot(normed, key_mat, preferred_element_type=jnp.float32)
    value_low = (
        jnp.dot(normed, value_mat, preferred_element_type=jnp.float32)
        .astype(jnp.bfloat16)
        .reshape(seq_count, span_len, KV_HEADS * HEAD_DIM)
    )
    own_span = lax.dynamic_index_in_dim(micro_order, ctx_index, axis=1, keepdims=False)
    offsets = jnp.arange(span_len, dtype=jnp.int32)
    query_pos = own_span[:, None] * span_len + offsets[None, :]
    key_pos = (micro_order[:, :, None] * span_len + offsets[None, None, :]).reshape(
        seq_count, ctx_parts * span_len
    )
    cos_table, sin_table = angle_tables(query_pos)
    query_rot = rotate(
        query_pre.reshape(seq_count, span_len, HEADS, HEAD_DIM), cos_table, sin_table
    ).astype(jnp.bfloat16)
    key_rot = (
        rotate(key_pre.reshape(seq_count, span_len, KV_HEADS, HEAD_DIM), cos_table, sin_table)
        .astype(jnp.bfloat16)
        .reshape(seq_count, span_len, KV_HEADS * HEAD_DIM)
    )
    key_all, value_all = (
        lax.all_gather(key_rot, "ctx", axis=1, tiled=True),
        lax.all_gather(value_low, "ctx", axis=1, tiled=True),
    )
    scaled = masked_scores(query_rot, key_all, query_pos, key_pos)
    row_peak = jnp.max(scaled, axis=-1, keepdims=True)
    exponent = jnp.exp(scaled - row_peak)
    row_total = jnp.sum(exponent, axis=-1, keepdims=True)
    attn_probs = (exponent / row_total).astype(jnp.bfloat16)
    log_total = row_peak + jnp.log(row_total)
    value_heads = value_all.reshape(seq_count, value_all.shape[1], KV_HEADS, HEAD_DIM)
    mixed = (
        jnp.einsum("shgqk,skhd->sqhgd", attn_probs, value_heads, preferred_element_type=jnp.float32)
        .reshape(row_count, HEADS * HEAD_DIM)
        .astype(jnp.bfloat16)
    )
    middle = sequence + jnp.dot(mixed, output_mat, preferred_element_type=jnp.float32)
    inverse_two = lax.rsqrt(jnp.mean(middle * middle, axis=-1, keepdims=True) + EPSILON)
    norm_two = middle * inverse_two
    hidden = (norm_two * ffn_gain).astype(jnp.bfloat16)
    gate_act = jnp.dot(hidden, gate_mat, preferred_element_type=jnp.float32)
    up_act = jnp.dot(hidden, up_mat, preferred_element_type=jnp.float32)
    sigmoid_gate = jax.nn.sigmoid(gate_act)
    inner = (gate_act * sigmoid_gate * up_act).astype(jnp.bfloat16)
    result = middle + jnp.dot(inner, down_mat, preferred_element_type=jnp.float32)
    kept_state = (
        inverse_one,
        norm_one,
        normed,
        query_rot,
        key_all,
        value_all,
        query_pos,
        key_pos,
        cos_table,
        sin_table,
        log_total,
        mixed,
        inverse_two,
        norm_two,
        hidden,
        gate_act,
        up_act,
        sigmoid_gate,
        inner,
    )
    return (result.astype(jnp.bfloat16).reshape(seq_count, span_len, model_width), kept_state)


def backward_pass(micro_cot, kept_state, whole_set):
    query_mat, key_mat, value_mat, output_mat, gate_mat, up_mat, down_mat = whole_set[:7]
    attn_gain = whole_set[7].astype(jnp.float32)
    ffn_gain = whole_set[8].astype(jnp.float32)
    (
        inverse_one,
        norm_one,
        normed,
        query_rot,
        key_all,
        value_all,
        query_pos,
        key_pos,
        cos_table,
        sin_table,
        log_total,
        mixed,
        inverse_two,
        norm_two,
        hidden,
        gate_act,
        up_act,
        sigmoid_gate,
        inner,
    ) = kept_state
    seq_count, span_len, model_width = micro_cot.shape
    row_count = seq_count * span_len
    key_length = key_all.shape[1]
    group_size = HEADS // KV_HEADS
    cot_rows = micro_cot.reshape(row_count, model_width)
    d_inner = transposed_product(cot_rows, down_mat)
    silu_slope = sigmoid_gate + gate_act * sigmoid_gate * (1.0 - sigmoid_gate)
    d_gate = (d_inner * up_act * silu_slope).astype(jnp.bfloat16)
    d_up = (d_inner * (gate_act * sigmoid_gate)).astype(jnp.bfloat16)
    d_hidden = transposed_product(d_gate, gate_mat) + transposed_product(d_up, up_mat)
    ffn_gain_grad = jnp.sum(d_hidden * norm_two, axis=0)
    d_norm_two = d_hidden * ffn_gain
    d_middle = cot_rows.astype(jnp.float32) + inverse_two * (
        d_norm_two - norm_two * jnp.mean(d_norm_two * norm_two, axis=-1, keepdims=True)
    )
    d_branch = d_middle.astype(jnp.bfloat16)
    d_mixed = (
        transposed_product(d_branch, output_mat)
        .astype(jnp.bfloat16)
        .reshape(seq_count, span_len, KV_HEADS, group_size, HEAD_DIM)
    )
    scaled = masked_scores(query_rot, key_all, query_pos, key_pos)
    attn_probs = jnp.exp(scaled - log_total)
    probs_low = attn_probs.astype(jnp.bfloat16)
    value_heads = value_all.reshape(seq_count, key_length, KV_HEADS, HEAD_DIM)
    key_heads = key_all.reshape(seq_count, key_length, KV_HEADS, HEAD_DIM)
    query_groups = query_rot.reshape(seq_count, span_len, KV_HEADS, group_size, HEAD_DIM)
    d_probs = jnp.einsum(
        "sqhgd,skhd->shgqk", d_mixed, value_heads, preferred_element_type=jnp.float32
    )
    value_term = jnp.einsum(
        "shgqk,sqhgd->skhd", probs_low, d_mixed, preferred_element_type=jnp.float32
    )
    row_delta = jnp.sum(attn_probs * d_probs, axis=-1, keepdims=True)
    d_scores = (HEAD_DIM ** (-0.5) * (attn_probs * (d_probs - row_delta))).astype(jnp.bfloat16)
    d_query_rot = jnp.einsum(
        "shgqk,skhd->sqhgd", d_scores, key_heads, preferred_element_type=jnp.float32
    )
    key_term = jnp.einsum(
        "shgqk,sqhgd->skhd", d_scores, query_groups, preferred_element_type=jnp.float32
    )
    d_key_rot, d_value = (
        lax.psum_scatter(
            key_term.reshape(seq_count, key_length, KV_HEADS * HEAD_DIM).astype(jnp.bfloat16),
            "ctx",
            scatter_dimension=1,
            tiled=True,
        ).astype(jnp.float32),
        lax.psum_scatter(
            value_term.reshape(seq_count, key_length, KV_HEADS * HEAD_DIM).astype(jnp.bfloat16),
            "ctx",
            scatter_dimension=1,
            tiled=True,
        ).astype(jnp.float32),
    )
    d_query = (
        unrotate(d_query_rot.reshape(seq_count, span_len, HEADS, HEAD_DIM), cos_table, sin_table)
        .reshape(row_count, HEADS * HEAD_DIM)
        .astype(jnp.bfloat16)
    )
    d_key = (
        unrotate(d_key_rot.reshape(seq_count, span_len, KV_HEADS, HEAD_DIM), cos_table, sin_table)
        .reshape(row_count, KV_HEADS * HEAD_DIM)
        .astype(jnp.bfloat16)
    )
    d_value_low = d_value.reshape(row_count, KV_HEADS * HEAD_DIM).astype(jnp.bfloat16)
    d_normed = (
        transposed_product(d_query, query_mat)
        + transposed_product(d_key, key_mat)
        + transposed_product(d_value_low, value_mat)
    )
    attn_gain_grad = jnp.sum(d_normed * norm_one, axis=0)
    d_norm_one = d_normed * attn_gain
    d_tokens = d_middle + inverse_one * (
        d_norm_one - norm_one * jnp.mean(d_norm_one * norm_one, axis=-1, keepdims=True)
    )
    product_rows = (
        normed,
        jnp.concatenate([d_query, d_key, d_value_low], axis=1),
        mixed,
        d_branch,
        hidden,
        jnp.concatenate([d_gate, d_up], axis=1),
        inner,
        cot_rows,
    )
    return (
        d_tokens.reshape(seq_count, span_len, model_width),
        product_rows,
        attn_gain_grad,
        ffn_gain_grad,
    )


def per_device(
    tokens,
    span_order,
    cotangent,
    query_weight,
    key_weight,
    value_weight,
    output_weight,
    gate_weight,
    up_weight,
    down_weight,
    attention_gain,
    feedforward_gain,
):
    ctx_index = lax.axis_index("ctx")
    outputs_list = []
    grads_list = []
    rows_list = []
    attn_gain_total = None
    ffn_gain_total = None
    for micro_step in range(tokens.shape[0]):
        whole_set = gather_weights(
            query_weight,
            key_weight,
            value_weight,
            output_weight,
            gate_weight,
            up_weight,
            down_weight,
            attention_gain,
            feedforward_gain,
        )
        layer_out, kept_state = forward_pass(
            tokens[micro_step], span_order[micro_step], whole_set, ctx_index
        )
        token_grad, product_rows, attn_gain_grad, ffn_gain_grad = backward_pass(
            cotangent[micro_step], kept_state, whole_set
        )
        outputs_list.append(layer_out)
        grads_list.append(token_grad)
        rows_list.append(product_rows)
        if attn_gain_total is None:
            attn_gain_total = attn_gain_grad
            ffn_gain_total = ffn_gain_grad
        else:
            attn_gain_total = attn_gain_total + attn_gain_grad
            ffn_gain_total = ffn_gain_total + ffn_gain_grad
    joined = [
        jnp.concatenate([rows_item[index] for rows_item in rows_list], axis=0) for index in range(8)
    ]
    query_width = query_weight.shape[1] * lax.axis_size("ctx")
    kv_width = key_weight.shape[1] * lax.axis_size("ctx")
    ff_width = gate_weight.shape[1] * lax.axis_size("ctx")
    attn_in_grad = rows_product(joined[0], joined[1])
    output_grad = rows_product(joined[2], joined[3])
    ffn_in_grad = rows_product(joined[4], joined[5])
    down_grad = rows_product(joined[6], joined[7])
    query_grad = attn_in_grad[:, :query_width]
    key_grad = attn_in_grad[:, query_width : query_width + kv_width]
    value_grad = attn_in_grad[:, query_width + kv_width :]
    gate_grad = ffn_in_grad[:, :ff_width]
    up_grad = ffn_in_grad[:, ff_width:]
    row_parts = (
        lax.psum_scatter(
            query_grad.astype(jnp.bfloat16), "dp", scatter_dimension=0, tiled=True
        ).astype(jnp.float32),
        lax.psum_scatter(
            key_grad.astype(jnp.bfloat16), "dp", scatter_dimension=0, tiled=True
        ).astype(jnp.float32),
        lax.psum_scatter(
            value_grad.astype(jnp.bfloat16), "dp", scatter_dimension=0, tiled=True
        ).astype(jnp.float32),
        lax.psum_scatter(
            output_grad.astype(jnp.bfloat16), "dp", scatter_dimension=0, tiled=True
        ).astype(jnp.float32),
        lax.psum_scatter(
            gate_grad.astype(jnp.bfloat16), "dp", scatter_dimension=0, tiled=True
        ).astype(jnp.float32),
        lax.psum_scatter(
            up_grad.astype(jnp.bfloat16), "dp", scatter_dimension=0, tiled=True
        ).astype(jnp.float32),
        lax.psum_scatter(
            down_grad.astype(jnp.bfloat16), "dp", scatter_dimension=0, tiled=True
        ).astype(jnp.float32),
        lax.psum_scatter(
            attn_gain_total.astype(jnp.bfloat16), "dp", scatter_dimension=0, tiled=True
        ).astype(jnp.float32),
        lax.psum_scatter(
            ffn_gain_total.astype(jnp.bfloat16), "dp", scatter_dimension=0, tiled=True
        ).astype(jnp.float32),
    )
    final_mats = (
        lax.psum_scatter(
            row_parts[0].astype(jnp.bfloat16), "ctx", scatter_dimension=1, tiled=True
        ).astype(jnp.float32),
        lax.psum_scatter(
            row_parts[1].astype(jnp.bfloat16), "ctx", scatter_dimension=1, tiled=True
        ).astype(jnp.float32),
        lax.psum_scatter(
            row_parts[2].astype(jnp.bfloat16), "ctx", scatter_dimension=1, tiled=True
        ).astype(jnp.float32),
        lax.psum_scatter(
            row_parts[3].astype(jnp.bfloat16), "ctx", scatter_dimension=1, tiled=True
        ).astype(jnp.float32),
        lax.psum_scatter(
            row_parts[4].astype(jnp.bfloat16), "ctx", scatter_dimension=1, tiled=True
        ).astype(jnp.float32),
        lax.psum_scatter(
            row_parts[5].astype(jnp.bfloat16), "ctx", scatter_dimension=1, tiled=True
        ).astype(jnp.float32),
        lax.psum_scatter(
            row_parts[6].astype(jnp.bfloat16), "ctx", scatter_dimension=1, tiled=True
        ).astype(jnp.float32),
    )
    final_gains = lax.psum((row_parts[7], row_parts[8]), "ctx")
    layer_output = jnp.stack(outputs_list, axis=0)
    input_grad = jnp.stack(grads_list, axis=0)
    return (
        layer_output,
        input_grad,
        final_mats[0],
        final_mats[1],
        final_mats[2],
        final_mats[3],
        final_mats[4],
        final_mats[5],
        final_mats[6],
        final_gains[0],
        final_gains[1],
    )


def solution(mesh):
    in_specs = (
        P(None, "dp", "ctx", None),
        P(None, "dp", None),
        P(None, "dp", "ctx", None),
        P("dp", "ctx"),
        P("dp", "ctx"),
        P("dp", "ctx"),
        P("dp", "ctx"),
        P("dp", "ctx"),
        P("dp", "ctx"),
        P("dp", "ctx"),
        P("dp"),
        P("dp"),
    )
    out_specs = (
        P(None, "dp", "ctx", None),
        P(None, "dp", "ctx", None),
        P("dp", "ctx"),
        P("dp", "ctx"),
        P("dp", "ctx"),
        P("dp", "ctx"),
        P("dp", "ctx"),
        P("dp", "ctx"),
        P("dp", "ctx"),
        P("dp"),
        P("dp"),
    )
    return jax.shard_map(
        per_device, mesh=mesh, in_specs=in_specs, out_specs=out_specs, check_vma=False
    )
```

profile of v0, /device:TPU:0, one launch (start us, length us, event | category | flops | bytes accessed | tf_op | source)
XLA Modules:
  0.0 813.6 jit_solution(11388998027127252122)
XLA Ops:
  7.2 17.5 %all_gather.90 = bf16[72,1536]{1,0:T(8,128)(2,1)} all-gather(bf16[72,384]{1,0:T(8,128)(2,1)} %param.20), channel_id=1, replica_groups=mesh['dp'=8,'ctx'=4] {'ctx'}, dimensions={1}, use_global_device_ids=true | all-gather | bytes 276480 | tf_op jit(solution)/shard_map/all_gather | solution.py:76
  24.8 15.0 %all_gather.88 = bf16[72,1536]{1,0:T(8,128)(2,1)} all-gather(bf16[72,384]{1,0:T(8,128)(2,1)} %param.19), channel_id=1, replica_groups=mesh['dp'=8,'ctx'=4] {'ctx'}, dimensions={1}, use_global_device_ids=true | all-gather | bytes 276480 | tf_op jit(solution)/shard_map/all_gather | solution.py:75
  39.8 14.2 %all_gather.92 = bf16[192,576]{0,1:T(8,128)(2,1)S(1)} all-gather(bf16[192,144]{0,1:T(8,128)(2,1)} %param.21), channel_id=1, replica_groups=mesh['dp'=8,'ctx'=4] {'ctx'}, dimensions={1}, use_global_device_ids=true | all-gather | bytes 276480 | tf_op jit(solution)/shard_map/all_gather | solution.py:77
  65.9 12.2 %all-reduce.8 = (bf16[576]{0:T(1024)(128)(2,1)S(1)}, bf16[576]{0:T(1024)(128)(2,1)S(1)}) all-reduce(bf16[576]{0:T(1024)(128)(2,1)S(1)} %dynamic-update-slice, bf16[576]{0:T(1024)(128)(2,1)S(1)} %dynamic-update-slice.1), channel_id=1, replica_groups=mesh['dp'=8,'ctx'=4] {'dp'}, use_global_device_ids=true, to_apply=%add | all-reduce | flops 1152 | bytes 4608
  78.2 13.1 %all_gather.80 = bf16[72,192]{0,1:T(8,128)(2,1)S(1)} all-gather(bf16[72,48]{0,1:T(8,128)(2,1)S(1)} %copy-done.79), channel_id=1, replica_groups=mesh['dp'=8,'ctx'=4] {'ctx'}, dimensions={1}, use_global_device_ids=true | all-gather | bytes 34560 | tf_op jit(solution)/shard_map/all_gather | solution.py:72
  91.4 9.5 %all_gather.81 = bf16[576,192]{1,0:T(8,128)(2,1)S(1)} all-gather(bf16[72,192]{1,0:T(8,128)(2,1)S(1)} %copy.53), channel_id=1, replica_groups=mesh['dp'=8,'ctx'=4] {'dp'}, dimensions={0}, use_global_device_ids=true | all-gather | bytes 248832 | tf_op jit(solution)/shard_map/all_gather | solution.py:81
  104.1 13.4 %all_gather.83 = bf16[72,576]{0,1:T(8,128)(2,1)S(1)} all-gather(bf16[72,144]{0,1:T(8,128)(2,1)S(1)} %copy.55), channel_id=1, replica_groups=mesh['dp'=8,'ctx'=4] {'ctx'}, dimensions={1}, use_global_device_ids=true | all-gather | bytes 103680 | tf_op jit(solution)/shard_map/all_gather | solution.py:71
  117.7 9.3 %all_gather.84 = bf16[576,576]{1,0:T(8,128)(2,1)S(1)} all-gather(bf16[72,576]{1,0:T(8,128)(2,1)S(1)} %copy.56), channel_id=1, replica_groups=mesh['dp'=8,'ctx'=4] {'dp'}, dimensions={0}, use_global_device_ids=true | all-gather | bytes 746496 | tf_op jit(solution)/shard_map/all_gather | solution.py:80
  129.3 13.3 %all_gather.77 = bf16[72,192]{0,1:T(8,128)(2,1)S(1)} all-gather(bf16[72,48]{0,1:T(8,128)(2,1)} %param.17), channel_id=1, replica_groups=mesh['dp'=8,'ctx'=4] {'ctx'}, dimensions={1}, use_global_device_ids=true | all-gather | bytes 34560 | tf_op jit(solution)/shard_map/all_gather | solution.py:73
  142.7 13.6 %all_gather.85 = bf16[72,576]{0,1:T(8,128)(2,1)S(1)} all-gather(bf16[72,144]{0,1:T(8,128)(2,1)S(1)} %copy.59), channel_id=1, replica_groups=mesh['dp'=8,'ctx'=4] {'ctx'}, dimensions={1}, use_global_device_ids=true | all-gather | bytes 103680 | tf_op jit(solution)/shard_map/all_gather | solution.py:74
  156.4 9.7 %all_gather.78 = bf16[576,192]{1,0:T(8,128)(2,1)S(1)} all-gather(bf16[72,192]{1,0:T(8,128)(2,1)S(1)} %copy.52), channel_id=1, replica_groups=mesh['dp'=8,'ctx'=4] {'dp'}, dimensions={0}, use_global_device_ids=true | all-gather | bytes 248832 | tf_op jit(solution)/shard_map/all_gather | solution.py:82
  168.2 14.7 %all_gather.95 = bf16[1,1024,192]{1,2,0:T(8,128)(2,1)S(1)} all-gather(bf16[1,256,192]{1,2,0:T(8,128)(2,1)S(1)} %bitcast.444), channel_id=1, replica_groups=mesh['dp'=8,'ctx'=4] {'ctx'}, dimensions={1}, use_global_device_ids=true | all-gather | bytes 491520 | tf_op jit(solution)/shard_map/all_gather | solution.py:139
  184.1 15.1 %all_gather.82 = bf16[1,1024,192]{1,2,0:T(8,128)(2,1)S(1)} all-gather(bf16[1,256,192]{1,2,0:T(8,128)(2,1)S(1)} %bitcast.445), channel_id=1, replica_groups=mesh['dp'=8,'ctx'=4] {'ctx'}, dimensions={1}, use_global_device_ids=true | all-gather | bytes 491520 | tf_op jit(solution)/shard_map/all_gather | solution.py:139
  199.8 14.7 %all-gather.1 = bf16[1024,192]{0,1:T(8,128)(2,1)S(1)} all-gather(bf16[256,192]{0,1:T(8,128)(2,1)S(1)} %convolution_convert_fusion.6), channel_id=3, replica_groups=mesh['dp'=8,'ctx'=4] {'ctx'}, dimensions={0}, use_global_device_ids=true | all-gather | bytes 491520 | tf_op jit(solution)/shard_map/all_gather | solution.py:140
  214.5 14.4 %all-gather = bf16[1024,192]{0,1:T(8,128)(2,1)S(1)} all-gather(bf16[256,192]{0,1:T(8,128)(2,1)S(1)} %convolution_convert_fusion.7), channel_id=2, replica_groups=mesh['dp'=8,'ctx'=4] {'ctx'}, dimensions={0}, use_global_device_ids=true | all-gather | bytes 491520 | tf_op jit(solution)/shard_map/all_gather | solution.py:140
  228.9 9.6 %all_gather.86 = bf16[576,576]{1,0:T(8,128)(2,1)S(1)} all-gather(bf16[72,576]{1,0:T(8,128)(2,1)S(1)} %copy.60), channel_id=1, replica_groups=mesh['dp'=8,'ctx'=4] {'dp'}, dimensions={0}, use_global_device_ids=true | all-gather | bytes 746496 | tf_op jit(solution)/shard_map/all_gather | solution.py:83
  255.7 3.5 fusion.153
  259.2 3.7 fusion.152
  262.9 4.8 multiply_convert_fusion.2
  280.0 4.7 fusion
  284.7 10.8 %fusion.19 = bf16[3,3,256,1024]{2,3,1,0:T(8,128)(2,1)} fusion(f32[3,1024,256,3]{2,1,3,0:T(8,128)} %get-tuple-element.120, f32[1,3,3,256,1024]{3,4,2,1,0:T(8,128)} %copy-done, f32[3,3,256]{2,1,0:T(4,128)S(1)} %get-tuple-element.119, f32[3,3,256]{2,1,0:T(4,128)S(1)} %log_add_fusion), kind=kLoop, calls=%fused_computation.29 | loop fusion | flops 11796480 | bytes 23611392 | tf_op jit(solution)/shard_map/reshape.125
  295.5 4.7 fusion.43
  300.5 7.0 fusion.4
  307.5 10.6 %fusion.18 = bf16[3,3,256,1024]{2,3,1,0:T(8,128)(2,1)} fusion(f32[3,1024,256,3]{2,1,3,0:T(8,128)} %get-tuple-element.122, f32[1,3,3,256,1024]{3,4,2,1,0:T(8,128)} %copy-done.1, f32[3,3,256]{2,1,0:T(4,128)S(1)} %get-tuple-element.121, f32[3,3,256]{2,1,0:T(4,128)S(1)} %copy-done.63), kind=kLoop, calls=%fused_computation.28 | loop fusion | flops 11796480 | bytes 23611392 | tf_op jit(solution)/shard_map/reshape.111
  318.1 4.6 fusion.42
  322.8 6.0 fusion.47
  332.3 6.0 fusion.44
  341.2 3.3 fusion.157
  348.1 16.7 %reduce-scatter.39.cloned.1.call-done = bf16[1,256,192]{1,2,0:T(8,128)(2,1)} async-done(((bf16[1,1024,192]{1,2,0:T(8,128)(2,1)}), bf16[1,256,192]{1,2,0:T(8,128)(2,1)}) %reduce-scatter.39.cloned.1.call-update) | async-done | bytes 98320 | tf_op jit(solution)/shard_map/reduce_scatter | solution.py:260
  364.8 21.3 %reduce-scatter.43.cloned.1.call-done = bf16[1,256,192]{1,2,0:T(8,128)(2,1)} async-done(((bf16[1,1024,192]{1,2,0:T(8,128)(2,1)}), bf16[1,256,192]{1,2,0:T(8,128)(2,1)}) %reduce-scatter.43.cloned.1.call-update) | async-done | bytes 98320 | tf_op jit(solution)/shard_map/reduce_scatter | solution.py:260
  390.7 3.8 convolution_convert_fusion
  397.8 4.1 convolution_convert_fusion.1
  411.1 10.8 %reduce-scatter.71.cloned.1.call-done = bf16[72,576]{1,0:T(8,128)(2,1)} async-done(((bf16[576,576]{1,0:T(8,128)(2,1)}), bf16[72,576]{1,0:T(8,128)(2,1)}) %reduce-scatter.71.cloned.1.call-update) | async-done | bytes 82960
  426.1 31.9 %reduce-scatter.45.cloned.1.call-done = bf16[72,192]{1,0:T(8,128)(2,1)} async-done(((bf16[576,192]{1,0:T(8,128)(2,1)}), bf16[72,192]{1,0:T(8,128)(2,1)}) %reduce-scatter.45.cloned.1.call-update) | async-done | bytes 27664 | tf_op jit(solution)/shard_map/reduce_scatter | solution.py:372
  461.6 32.1 %reduce-scatter.47.cloned.1.call-done = bf16[72,192]{1,0:T(8,128)(2,1)} async-done(((bf16[576,192]{1,0:T(8,128)(2,1)}), bf16[72,192]{1,0:T(8,128)(2,1)}) %reduce-scatter.47.cloned.1.call-update) | async-done | bytes 27664 | tf_op jit(solution)/shard_map/reduce_scatter | solution.py:375
  497.8 33.5 %reduce-scatter.69.cloned.1.call-done = bf16[72,576]{1,0:T(8,128)(2,1)} async-done(((bf16[576,576]{1,0:T(8,128)(2,1)}), bf16[72,576]{1,0:T(8,128)(2,1)}) %reduce-scatter.69.cloned.1.call-update) | async-done | bytes 82960
  533.1 12.5 %all-reduce.7 = (bf16[576]{0:T(1024)(128)(2,1)S(1)}, bf16[576]{0:T(1024)(128)(2,1)S(1)}) all-reduce(bf16[576]{0:T(1024)(128)(2,1)S(1)} %add_convert_fusion.9, bf16[576]{0:T(1024)(128)(2,1)S(1)} %add_convert_fusion.8), channel_id=22, replica_groups=mesh['dp'=8,'ctx'=4] {'dp'}, use_global_device_ids=true, to_apply=%region_34.35.clone | all-reduce | flops 1152 | bytes 4608
  545.6 28.4 %reduce-scatter.49.cloned.1.call-done = bf16[72,1536]{1,0:T(8,128)(2,1)} async-done(((bf16[576,1536]{1,0:T(8,128)(2,1)}), bf16[72,1536]{1,0:T(8,128)(2,1)}) %reduce-scatter.49.cloned.1.call-update) | async-done | bytes 221200 | tf_op jit(solution)/shard_map/reduce_scatter | solution.py:381
  575.9 40.8 %reduce-scatter.51.cloned.1.call-done = bf16[72,1536]{1,0:T(8,128)(2,1)} async-done(((bf16[576,1536]{1,0:T(8,128)(2,1)}), bf16[72,1536]{1,0:T(8,128)(2,1)}) %reduce-scatter.51.cloned.1.call-update) | async-done | bytes 221200 | tf_op jit(solution)/shard_map/reduce_scatter | solution.py:384
  621.1 39.3 %reduce-scatter.53.cloned.1.call-done = bf16[192,576]{1,0:T(8,128)(2,1)} async-done(((bf16[1536,576]{1,0:T(8,128)(2,1)}), bf16[192,576]{1,0:T(8,128)(2,1)}) %reduce-scatter.53.cloned.1.call-update) | async-done | bytes 221200 | tf_op jit(solution)/shard_map/reduce_scatter | solution.py:387
  662.2 12.3 %all-reduce.6 = (f32[72]{0:T(128)}, f32[72]{0:T(128)}) all-reduce(f32[72]{0:T(128)S(1)} %dynamic-slice_convert_fusion.1, f32[72]{0:T(128)S(1)} %dynamic-slice_convert_fusion), channel_id=1, replica_groups=mesh['dp'=8,'ctx'=4] {'ctx'}, use_global_device_ids=true, to_apply=%region_35.36 | all-reduce | flops 144 | bytes 1152 | tf_op jit(solution)/shard_map/psum | solution.py:420
  677.1 4.8 reduce-scatter.61.cloned.1.call-done
  683.3 18.4 %reduce-scatter.57.cloned.1.call-done = bf16[48,72]{1,0:T(8,128)(2,1)} async-done(((bf16[192,72]{1,0:T(8,128)(2,1)}), bf16[48,72]{1,0:T(8,128)(2,1)}) %reduce-scatter.57.cloned.1.call-update) | async-done | bytes 6928
  703.2 18.5 %reduce-scatter.59.cloned.1.call-done = bf16[48,72]{1,0:T(8,128)(2,1)} async-done(((bf16[192,72]{1,0:T(8,128)(2,1)}), bf16[48,72]{1,0:T(8,128)(2,1)}) %reduce-scatter.59.cloned.1.call-update) | async-done | bytes 6928
  723.2 18.6 %reduce-scatter.55.cloned.1.call-done = bf16[144,72]{1,0:T(8,128)(2,1)} async-done(((bf16[576,72]{1,0:T(8,128)(2,1)}), bf16[144,72]{1,0:T(8,128)(2,1)}) %reduce-scatter.55.cloned.1.call-update) | async-done | bytes 20752
  743.3 19.7 %reduce-scatter.63.cloned.1.call-done = bf16[384,72]{1,0:T(8,128)(2,1)} async-done(((bf16[1536,72]{1,0:T(8,128)(2,1)}), bf16[384,72]{1,0:T(8,128)(2,1)}) %reduce-scatter.63.cloned.1.call-update) | async-done | bytes 55312
  764.7 19.3 %reduce-scatter.65.cloned.1.call-done = bf16[384,72]{1,0:T(8,128)(2,1)} async-done(((bf16[1536,72]{1,0:T(8,128)(2,1)}), bf16[384,72]{1,0:T(8,128)(2,1)}) %reduce-scatter.65.cloned.1.call-update) | async-done | bytes 55312
  785.7 18.9 %reduce-scatter.67.cloned.1.call-done = bf16[144,192]{1,0:T(8,128)(2,1)} async-done(((bf16[576,192]{1,0:T(8,128)(2,1)}), bf16[144,192]{1,0:T(8,128)(2,1)}) %reduce-scatter.67.cloned.1.call-update) | async-done | bytes 55312
  (357 shorter events, 111.7 us)
Async XLA Ops:
  7.2 70.9 %copy-start.6 = (bf16[2,1,256,576]{2,3,1,0:T(8,128)(2,1)S(1)}, bf16[2,1,256,576]{2,3,1,0:T(8,128)(2,1)}, u32[]{:S(2)}) copy-start(bf16[2,1,256,576]{2,3,1,0:T(8,128)(2,1)} %param.12) | copy-start | bytes 1769476
  7.2 71.0 %copy-start.79 = (bf16[72,48]{0,1:T(8,128)(2,1)S(1)}, bf16[72,48]{0,1:T(8,128)(2,1)}, u32[]{:S(2)}) copy-start(bf16[72,48]{0,1:T(8,128)(2,1)} %param.16) | copy-start | bytes 20740
  7.2 248.5 %all-gather.8.cloned.1.call-start = ((), (), s32[]{:S(2)}) async-start(), calls=%async_computation.19 | async-start | bytes 1990656 | tf_op jit(solution)/shard_map/all_gather | solution.py:85
  24.8 234.4 %all-gather.6.cloned.1.call-start = ((), (), s32[]{:S(2)}) async-start(), calls=%async_computation.18 | async-start | bytes 1990656 | tf_op jit(solution)/shard_map/all_gather | solution.py:84
  39.8 223.1 %all-gather.10.cloned.1.call-start = ((), (), s32[]{:S(2)}) async-start(), calls=%async_computation.20 | async-start | bytes 2211840 | tf_op jit(solution)/shard_map/all_gather | solution.py:86
  54.9 289.8 %reduce-scatter.41.cloned.1.call-start = ((), (), s32[]{:S(2)}) async-start(), calls=%async_computation.23 | async-start | bytes 491520 | tf_op jit(solution)/shard_map/reduce_scatter | solution.py:254
  78.1 49.8 %copy-start.64 = (f32[576]{0:T(1024)}, f32[576]{0:T(1024)S(1)}, u32[]{:S(2)}) copy-start(f32[576]{0:T(1024)S(1)} %convert_element_type.460) | copy-start | bytes 6916
  104.0 95.2 %copy-start.37 = (bf16[256,576]{0,1:T(8,128)(2,1)}, bf16[256,576]{0,1:T(8,128)(2,1)S(1)}, u32[]{:S(2)}) copy-start(bf16[256,576]{0,1:T(8,128)(2,1)S(1)} %get-tuple-element.82) | copy-start | bytes 884740
  128.4 71.1 %copy-start.38 = (bf16[256,576]{0,1:T(8,128)(2,1)S(1)}, bf16[256,576]{0,1:T(8,128)(2,1)}, u32[]{:S(2)}) copy-start(bf16[256,576]{0,1:T(8,128)(2,1)} %get-tuple-element.83) | copy-start | bytes 884740
  166.1 48.5 %copy-start.18 = (bf16[576,192]{1,0:T(8,128)(2,1)}, bf16[576,192]{1,0:T(8,128)(2,1)S(1)}, u32[]{:S(2)}) copy-start(bf16[576,192]{1,0:T(8,128)(2,1)S(1)} %all_gather.78) | copy-start | bytes 663556
  167.2 71.4 %copy-start.43 = (f32[256,32]{0,1:T(8,128)}, f32[256,32]{0,1:T(8,128)S(1)}, u32[]{:S(2)}) copy-start(f32[256,32]{0,1:T(8,128)S(1)} %get-tuple-element.107) | copy-start | bytes 98308
  167.2 71.4 %copy-start.45 = (f32[256,32]{0,1:T(8,128)}, f32[256,32]{0,1:T(8,128)S(1)}, u32[]{:S(2)}) copy-start(f32[256,32]{0,1:T(8,128)S(1)} %get-tuple-element.108) | copy-start | bytes 98308
  167.2 71.4 %copy-start.39 = (f32[256,32]{0,1:T(8,128)}, f32[256,32]{0,1:T(8,128)S(1)}, u32[]{:S(2)}) copy-start(f32[256,32]{0,1:T(8,128)S(1)} %get-tuple-element.97) | copy-start | bytes 98308
  167.2 71.4 %copy-start.41 = (f32[256,32]{0,1:T(8,128)}, f32[256,32]{0,1:T(8,128)S(1)}, u32[]{:S(2)}) copy-start(f32[256,32]{0,1:T(8,128)S(1)} %get-tuple-element.98) | copy-start | bytes 98308
  182.9 56.3 %copy-start.27 = (bf16[1,1024,192]{1,2,0:T(8,128)(2,1)}, bf16[1,1024,192]{1,2,0:T(8,128)(2,1)S(1)}, u32[]{:S(2)}) copy-start(bf16[1,1024,192]{1,2,0:T(8,128)(2,1)S(1)} %all_gather.95) | copy-start | bytes 1179652
  199.2 48.2 %copy-start.25 = (bf16[1,1024,192]{1,2,0:T(8,128)(2,1)}, bf16[1,1024,192]{1,2,0:T(8,128)(2,1)S(1)}, u32[]{:S(2)}) copy-start(bf16[1,1024,192]{1,2,0:T(8,128)(2,1)S(1)} %all_gather.82) | copy-start | bytes 1179652
  199.5 39.4 %copy-start.84 = (s32[4]{0:T(128)S(1)}, s32[4]{0:T(128)}, u32[]{:S(2)}) copy-start(s32[4]{0:T(128)} %get-tuple-element.102) | copy-start | bytes 52
  199.5 39.5 %copy-start.87 = (s32[256]{0:T(256)S(1)}, s32[256]{0:T(256)}, u32[]{:S(2)}) copy-start(s32[256]{0:T(256)} %iota_add_fusion) | copy-start | bytes 3076
  300.2 45.6 %reduce-scatter.37.cloned.1.call-start = ((), (), s32[]{:S(2)}) async-start(), calls=%async_computation.21 | async-start | bytes 491520 | tf_op jit(solution)/shard_map/reduce_scatter | solution.py:254
  322.8 42.0 %reduce-scatter.39.cloned.1.call-start = ((), (), s32[]{:S(2)}) async-start(), calls=%async_computation.22 | async-start | bytes 491520 | tf_op jit(solution)/shard_map/reduce_scatter | solution.py:260
  328.9 57.1 %reduce-scatter.43.cloned.1.call-start = ((), (), s32[]{:S(2)}) async-start(), calls=%async_computation.24 | async-start | bytes 491520 | tf_op jit(solution)/shard_map/reduce_scatter | solution.py:260
  338.3 83.6 %reduce-scatter.71.cloned.1.call-start = ((), (), s32[]{:S(2)}) async-start(), calls=%async_computation.38 | async-start | bytes 829440
  344.6 113.3 %reduce-scatter.45.cloned.1.call-start = ((), (), s32[]{:S(2)}) async-start(), calls=%async_computation.25 | async-start | bytes 331776 | tf_op jit(solution)/shard_map/reduce_scatter | solution.py:372
  344.7 41.4 %copy-start.34 = (bf16[1,256,9,64]{1,3,2,0:T(8,128)(2,1)}, bf16[1,256,9,64]{1,3,2,0:T(8,128)(2,1)S(1)}, u32[]{:S(2)}) copy-start(bf16[1,256,9,64]{1,3,2,0:T(8,128)(2,1)S(1)} %pad_maximum_fusion.5) | copy-start | bytes 884740
  344.7 41.3 %copy-start.33 = (bf16[1,256,9,64]{1,3,2,0:T(8,128)(2,1)}, bf16[1,256,9,64]{1,3,2,0:T(8,128)(2,1)S(1)}, u32[]{:S(2)}) copy-start(bf16[1,256,9,64]{1,3,2,0:T(8,128)(2,1)S(1)} %pad_maximum_fusion.4) | copy-start | bytes 884740
  389.0 104.7 %reduce-scatter.47.cloned.1.call-start = ((), (), s32[]{:S(2)}) async-start(), calls=%async_computation.26 | async-start | bytes 331776 | tf_op jit(solution)/shard_map/reduce_scatter | solution.py:375
  389.6 141.7 %reduce-scatter.69.cloned.1.call-start = ((), (), s32[]{:S(2)}) async-start(), calls=%async_computation.37 | async-start | bytes 829440
  390.6 183.3 %reduce-scatter.49.cloned.1.call-start = ((), (), s32[]{:S(2)}) async-start(), calls=%async_computation.27 | async-start | bytes 1990656 | tf_op jit(solution)/shard_map/reduce_scatter | solution.py:381
  396.7 220.1 %reduce-scatter.51.cloned.1.call-start = ((), (), s32[]{:S(2)}) async-start(), calls=%async_computation.28 | async-start | bytes 1990656 | tf_op jit(solution)/shard_map/reduce_scatter | solution.py:384
  397.4 262.9 %reduce-scatter.53.cloned.1.call-start = ((), (), s32[]{:S(2)}) async-start(), calls=%async_computation.29 | async-start | bytes 2211840 | tf_op jit(solution)/shard_map/reduce_scatter | solution.py:387
  402.0 279.9 %reduce-scatter.61.cloned.1.call-start = ((), (), s32[]{:S(2)}) async-start(), calls=%async_computation.33 | async-start | bytes 184320
  409.9 49.6 %copy-start.19 = (bf16[576,192]{1,0:T(8,128)(2,1)S(1)}, bf16[576,192]{1,0:T(8,128)(2,1)}, u32[]{:S(2)}) copy-start(bf16[576,192]{1,0:T(8,128)(2,1)} %copy-done.18) | copy-start | bytes 663556
  409.9 49.6 %copy-start.66 = (bf16[1,256,192]{1,2,0:T(8,128)(2,1)S(1)}, bf16[1,256,192]{1,2,0:T(8,128)(2,1)}, u32[]{:S(2)}) copy-start(bf16[1,256,192]{1,2,0:T(8,128)(2,1)} %reduce-scatter.43.cloned.1.call-done) | copy-start | bytes 294916
  411.1 84.2 %copy-start.65 = (f32[576]{0:T(1024)S(1)}, f32[576]{0:T(1024)}, u32[]{:S(2)}) copy-start(f32[576]{0:T(1024)} %copy-done.64) | copy-start | bytes 6916
  411.1 84.2 %copy-start.75 = (f32[256]{0:T(256)S(1)}, f32[256]{0:T(256)}, u32[]{:S(2)}) copy-start(f32[256]{0:T(256)} %copy-done.74) | copy-start | bytes 3076
  411.1 84.2 %copy-start.77 = (f32[256]{0:T(256)S(1)}, f32[256]{0:T(256)}, u32[]{:S(2)}) copy-start(f32[256]{0:T(256)} %copy-done.76) | copy-start | bytes 3076
  423.6 278.1 %reduce-scatter.57.cloned.1.call-start = ((), (), s32[]{:S(2)}) async-start(), calls=%async_computation.31 | async-start | bytes 61440
  459.4 262.3 %reduce-scatter.59.cloned.1.call-start = ((), (), s32[]{:S(2)}) async-start(), calls=%async_computation.32 | async-start | bytes 61440
  495.2 123.7 %copy-start.14 = (f32[256,576]{0,1:T(8,128)S(1)}, f32[256,576]{0,1:T(8,128)}, u32[]{:S(2)}) copy-start(f32[256,576]{0,1:T(8,128)} %copy-done.13) | copy-start | bytes 1769476
  495.2 123.7 %copy-start.68 = (f32[256]{0:T(256)S(1)}, f32[256]{0:T(256)}, u32[]{:S(2)}) copy-start(f32[256]{0:T(256)} %add_rsqrt_fusion) | copy-start | bytes 3076
  495.2 123.7 %copy-start.83 = (f32[256]{0:T(256)S(1)}, f32[256]{0:T(256)}, u32[]{:S(2)}) copy-start(f32[256]{0:T(256)} %copy-done.82) | copy-start | bytes 3076
  495.2 246.6 %reduce-scatter.55.cloned.1.call-start = ((), (), s32[]{:S(2)}) async-start(), calls=%async_computation.30 | async-start | bytes 184320
  533.0 230.0 %reduce-scatter.63.cloned.1.call-start = ((), (), s32[]{:S(2)}) async-start(), calls=%async_computation.34 | async-start | bytes 491520
  575.8 208.2 %reduce-scatter.65.cloned.1.call-start = ((), (), s32[]{:S(2)}) async-start(), calls=%async_computation.35 | async-start | bytes 491520
  575.9 98.5 %copy-start.72 = (f32[256]{0:T(256)S(1)}, f32[256]{0:T(256)}, u32[]{:S(2)}) copy-start(f32[256]{0:T(256)} %copy-done.70) | copy-start | bytes 3076
  575.9 98.5 %copy-start.81 = (f32[256]{0:T(256)S(1)}, f32[256]{0:T(256)}, u32[]{:S(2)}) copy-start(f32[256]{0:T(256)} %copy-done.80) | copy-start | bytes 3076
  618.7 185.9 %reduce-scatter.67.cloned.1.call-start = ((), (), s32[]{:S(2)}) async-start(), calls=%async_computation.36 | async-start | bytes 368640
  621.1 54.9 %copy-start.24 = (f32[1,1,256,576]{2,3,1,0:T(8,128)S(1)}, f32[1,1,256,576]{2,3,1,0:T(8,128)}, u32[]{:S(2)}) copy-start(f32[1,1,256,576]{2,3,1,0:T(8,128)} %fusion.101) | copy-start | bytes 1769476
  (64 other events, 435.5 us)
Sparse Core Ops, SparseCore 0:
  24.9 26.5 all-gather.7
  53.4 26.5 all-gather.5
  82.5 27.6 all-gather.9
  300.4 20.7 reduce-scatter.40
  323.4 20.4 reduce-scatter.36
  346.0 18.7 reduce-scatter.38
  367.2 18.8 reduce-scatter.42
  389.3 32.5 reduce-scatter.70
  425.0 32.8 reduce-scatter.44
  460.8 32.8 reduce-scatter.46
  496.9 34.3 reduce-scatter.68
  534.5 39.4 reduce-scatter.48
  577.3 39.3 reduce-scatter.50
  620.0 40.2 reduce-scatter.52
  662.5 19.2 reduce-scatter.60
  684.5 17.1 reduce-scatter.56
  704.5 17.1 reduce-scatter.58
  724.4 17.3 reduce-scatter.54
  744.2 18.7 reduce-scatter.62
  765.1 18.8 reduce-scatter.64
  786.4 18.1 reduce-scatter.66
where the time goes:
time: 822 us; the launch traced here: 814 us
  waiting for transfers between devices  374 us (45%)
  blocking collectives  234 us (28%)
  matrix products  98.4 us (12%)
  other arithmetic  49.6 us (6%)
  local copies, waits for them, and re-layouts  38.4 us (5%)
  between operations  17.4 us (2%)
    unnamed x30, waiting for transfers between devices  164 us
    reduce_scatter x1, waiting for transfers between devices, per_device(): lax.psum_scatter(up_grad.astype(jnp.bfloat16), 'dp', scatter_dimension=0,...  40.8 us
    reduce_scatter x1, waiting for transfers between devices, per_device(): lax.psum_scatter(down_grad.astype(jnp.bfloat16), 'dp', scatter_dimension=...  39.3 us
    reduce_scatter x2, waiting for transfers between devices, backward_pass(): lax.psum_scatter(value_term.reshape(seq_count, key_length, KV_HEADS * HEA...  38 us
    unnamed x208, local copies, waits for them, and re-layouts  32.4 us
    reduce_scatter x1, waiting for transfers between devices, per_device(): lax.psum_scatter(value_grad.astype(jnp.bfloat16), 'dp', scatter_dimension...  32.1 us
    reduce_scatter x1, waiting for transfers between devices, per_device(): lax.psum_scatter(key_grad.astype(jnp.bfloat16), 'dp', scatter_dimension=0...  31.9 us
    all_gather x2, blocking collectives, forward_pass(): lax.all_gather(key_rot, 'ctx', axis=1, tiled=True)  29.8 us
  transfers between devices with their start and end apart: 21, of which 16 were waited for; matrix products, arithmetic and copies ran while one was open for 18% of the time, Pallas kernels for 0%

commit v1 on v0

--- a/solution.py
+++ b/solution.py
@@ -1,6 +1,10 @@
+import functools
+
 import jax
 import jax.numpy as jnp
 from jax import lax
+from jax.experimental import pallas as pl
+from jax.experimental.pallas import tpu as pltpu
 from jax.sharding import PartitionSpec as P
 
 HEADS = 9
@@ -54,6 +58,314 @@
     return lax.dot_general(
         left_mat, right_mat, (((1,), (1,)), ((), ())), preferred_element_type=jnp.float32
     )
+
+
+MESH = pl.DeviceIdType.MESH
+VMEM_LIMIT = 56 * 1024 * 1024
+
+
+def place_on_slice():
+    part = lax.axis_index("dp")
+    return lax.axis_index("ctx"), part % 2, part // 4, (part // 2) % 2
+
+
+def device_at(ctx, core, row, col):
+    return (row * 4 + col * 2 + core, ctx)
+
+
+def greet(partners):
+    barrier = pltpu.get_barrier_semaphore()
+    for partner in partners:
+        pl.semaphore_signal(barrier, inc=1, device_id=partner, device_id_type=MESH)
+    pl.semaphore_wait(barrier, len(partners))
+
+
+def remote(source, target, send_sem, recv_sem, device):
+    return pltpu.make_async_remote_copy(
+        src_ref=source,
+        dst_ref=target,
+        send_sem=send_sem,
+        recv_sem=recv_sem,
+        device_id=device,
+        device_id_type=MESH,
+    )
+
+
+def gather_kernel(n_ctx, own_ref, all_ref, send_sem, recv_sem):
+    ctx, core, row, col = place_on_slice()
+    sibling = device_at(ctx, 1 - core, row, col)
+    beside = device_at(ctx, core, row, 1 - col)
+    across = device_at(ctx, core, 1 - row, col)
+    spans = [device_at((ctx + step) % n_ctx, core, row, col) for step in range(1, n_ctx)]
+    greet([sibling, beside, across] + spans)
+    sent = []
+
+    def send(source, target, group, index, device):
+        copy = remote(source, target, send_sem.at[group, index], recv_sem.at[group, index], device)
+        copy.start()
+        sent.append(copy)
+
+    def arrive(target, group, index):
+        remote(
+            target, target, send_sem.at[group, index], recv_sem.at[group, index], sibling
+        ).wait_recv()
+
+    for step in range(1, n_ctx):
+        send(own_ref, all_ref.at[ctx, core, row, col], 0, step, spans[step - 1])
+    all_ref[ctx, core, row, col] = own_ref[...]
+
+    def piece(step):
+        return (ctx + n_ctx - step) % n_ctx
+
+    def first(step):
+        at = piece(step)
+        if step:
+            arrive(all_ref.at[at, core, row, col], 0, step)
+        half_a, half_b = all_ref.at[at, core, row, col, 0], all_ref.at[at, core, row, col, 1]
+        send(half_a, half_a, 1, step, beside)
+        send(half_b, half_b, 2, step, across)
+
+    def second(step):
+        at = piece(step)
+        arrive(all_ref.at[at, core, row, 1 - col, 0], 1, step)
+        arrive(all_ref.at[at, core, 1 - row, col, 1], 2, step)
+        half_a, half_b = all_ref.at[at, core, row, :, 0], all_ref.at[at, core, :, col, 1]
+        send(half_a, half_a, 3, step, across)
+        send(half_b, half_b, 4, step, beside)
+
+    def third(step):
+        at = piece(step)
+        arrive(all_ref.at[at, core, 1 - row, :, 0], 3, step)
+        arrive(all_ref.at[at, core, :, 1 - col, 1], 4, step)
+        send(all_ref.at[at, core], all_ref.at[at, core], 5, step, sibling)
+
+    for tick in range(n_ctx + 2):
+        if 0 <= tick - 1 < n_ctx:
+            second(tick - 1)
+        if 0 <= tick - 2 < n_ctx:
+            third(tick - 2)
+        if tick < n_ctx:
+            first(tick)
+    for step in range(n_ctx):
+        arrive(all_ref.at[piece(step), 1 - core], 5, step)
+    for copy in sent:
+        copy.wait_send()
+
+
+def scatter_kernel(
+    n_ctx, term_ref, sum_ref, got_1, part_1, got_2, part_2, got_3, part_3, got_4, send_sem, recv_sem
+):
+    ctx, core, row, col = place_on_slice()
+    sibling = device_at(ctx, 1 - core, row, col)
+    beside = device_at(ctx, core, row, 1 - col)
+    across = device_at(ctx, core, 1 - row, col)
+    spans = [device_at((ctx + step) % n_ctx, core, row, col) for step in range(1, n_ctx)]
+    greet([sibling, beside, across] + spans)
+    order = list(range(1, n_ctx)) + [0]
+    sent = []
+
+    def send(source, target, group, index, device):
+        copy = remote(source, target, send_sem.at[group, index], recv_sem.at[group, index], device)
+        copy.start()
+        sent.append(copy)
+
+    def arrive(target, group, index):
+        remote(
+            target, target, send_sem.at[group, index], recv_sem.at[group, index], sibling
+        ).wait_recv()
+
+    def piece(step):
+        return (ctx + step) % n_ctx
+
+    def add(one, two):
+        return (one.astype(jnp.float32) + two.astype(jnp.float32)).astype(jnp.bfloat16)
+
+    for step in order:
+        send(term_ref.at[piece(step), 1 - core], got_1.at[step], 0, step, sibling)
+
+    def first(step):
+        at = piece(step)
+        arrive(got_1.at[step], 0, step)
+
+        def body(index, carry):
+            r, c, h = index // 4, (index // 2) % 2, index % 2
+            part_1[step, r, c, h] = add(term_ref[at, core, r, c, h], got_1[step, r, c, h])
+            return carry
+
+        lax.fori_loop(0, 8, body, 0)
+        send(part_1.at[step, :, 1 - col, 0], got_2.at[step, 0], 1, step, beside)
+        send(part_1.at[step, 1 - row, :, 1], got_2.at[step, 1], 2, step, across)
+
+    def second(step):
+        arrive(got_2.at[step, 0], 1, step)
+        arrive(got_2.at[step, 1], 2, step)
+        for index in range(2):
+            part_2[step, 0, index] = add(part_1[step, index, col, 0], got_2[step, 0, index])
+            part_2[step, 1, index] = add(part_1[step, row, index, 1], got_2[step, 1, index])
+        send(part_2.at[step, 0, 1 - row], got_3.at[step, 0], 3, step, across)
+        send(part_2.at[step, 1, 1 - col], got_3.at[step, 1], 4, step, beside)
+
+    def third(step):
+        arrive(got_3.at[step, 0], 3, step)
+        arrive(got_3.at[step, 1], 4, step)
+        part_3[step, 0] = add(part_2[step, 0, row], got_3[step, 0])
+        part_3[step, 1] = add(part_2[step, 1, col], got_3[step, 1])
+        if step:
+            send(part_3.at[step], got_4.at[step], 5, step, spans[step - 1])
+
+    for tick in range(n_ctx + 2):
+        if tick < n_ctx:
+            first(order[tick])
+        if 0 <= tick - 1 < n_ctx:
+            second(order[tick - 1])
+        if 0 <= tick - 2 < n_ctx:
+            third(order[tick - 2])
+    for step in range(1, n_ctx):
+        arrive(got_4.at[step], 5, step)
+    for half in range(2):
+        total = part_3[0, half].astype(jnp.float32)
+        for step in range(1, n_ctx):
+            total = total + got_4[step, half].astype(jnp.float32)
+        sum_ref[half] = total
+    for copy in sent:
+        copy.wait_send()
+
+
+def span_gather_kernel(n_ctx, own_ref, all_ref, send_sem, recv_sem):
+    ctx, core, row, col = place_on_slice()
+    spans = [device_at((ctx + step) % n_ctx, core, row, col) for step in range(1, n_ctx)]
+    greet(spans)
+    copies = []
+    for step in range(1, n_ctx):
+        copy = remote(
+            own_ref, all_ref.at[ctx], send_sem.at[step], recv_sem.at[step], spans[step - 1]
+        )
+        copy.start()
+        copies.append(copy)
+    all_ref[ctx] = own_ref[...]
+    for step in range(1, n_ctx):
+        target = all_ref.at[(ctx + n_ctx - step) % n_ctx]
+        remote(target, target, send_sem.at[step], recv_sem.at[step], spans[0]).wait_recv()
+    for copy in copies:
+        copy.wait_send()
+
+
+def span_scatter_kernel(n_ctx, term_ref, sum_ref, got_ref, send_sem, recv_sem):
+    ctx, core, row, col = place_on_slice()
+    spans = [device_at((ctx + step) % n_ctx, core, row, col) for step in range(1, n_ctx)]
+    greet(spans)
+    copies = []
+    for step in range(1, n_ctx):
+        copy = remote(
+            term_ref.at[(ctx + step) % n_ctx],
+            got_ref.at[step],
+            send_sem.at[step],
+            recv_sem.at[step],
+            spans[step - 1],
+        )
+        copy.start()
+        copies.append(copy)
+    for step in range(1, n_ctx):
+        copies[step - 1].wait_recv()
+    total = term_ref[ctx].astype(jnp.float32)
+    for step in range(1, n_ctx):
+        total = total + got_ref[step].astype(jnp.float32)
+    sum_ref[...] = total
+    for copy in copies:
+        copy.wait_send()
+
+
+def vmem_call(kernel, operand, out_shape, scratch, collective_id):
+    whole = pl.BlockSpec(memory_space=pltpu.VMEM)
+    return pl.pallas_call(
+        kernel,
+        out_shape=out_shape,
+        in_specs=[whole],
+        out_specs=whole,
+        scratch_shapes=scratch,
+        compiler_params=pltpu.CompilerParams(
+            collective_id=collective_id, has_side_effects=True, vmem_limit_bytes=VMEM_LIMIT
+        ),
+    )(operand)
+
+
+def own_plan():
+    return lax.axis_size("dp") == 8 and lax.axis_size("ctx") == 4
+
+
+def span_gather(own):
+    n_ctx = lax.axis_size("ctx")
+    if not own_plan():
+        return lax.all_gather(own, "ctx", axis=0)
+    seqs, span, features = own.shape
+    sems = pltpu.SemaphoreType.DMA((n_ctx,))
+    gathered = vmem_call(
+        functools.partial(span_gather_kernel, n_ctx),
+        own.reshape(seqs * span, features),
+        jax.ShapeDtypeStruct((n_ctx, seqs * span, features), own.dtype),
+        [sems, sems],
+        1,
+    )
+    return gathered.reshape(n_ctx, seqs, span, features)
+
+
+def span_scatter(terms):
+    n_ctx, seqs, span, features = terms.shape
+    if not own_plan():
+        return lax.psum_scatter(terms, "ctx", scatter_dimension=0).astype(jnp.float32)
+    sems = pltpu.SemaphoreType.DMA((n_ctx,))
+    summed = vmem_call(
+        functools.partial(span_scatter_kernel, n_ctx),
+        terms.reshape(n_ctx, seqs * span, features),
+        jax.ShapeDtypeStruct((seqs * span, features), jnp.float32),
+        [pltpu.VMEM((n_ctx, seqs * span, features), terms.dtype), sems, sems],
+        2,
+    )
+    return summed.reshape(seqs, span, features)
+
+
+def all_shards(packed):
+    n_dp, n_ctx = lax.axis_size("dp"), lax.axis_size("ctx")
+    if not own_plan():
+        return lax.all_gather(packed, ("dp", "ctx"), axis=0).reshape(n_dp, n_ctx, *packed.shape)
+    sems = pltpu.SemaphoreType.DMA((6, n_ctx))
+    gathered = vmem_call(
+        functools.partial(gather_kernel, n_ctx),
+        packed,
+        jax.ShapeDtypeStruct((n_ctx, 2, 2, 2) + packed.shape, packed.dtype),
+        [sems, sems],
+        3,
+    )
+    return gathered.transpose(2, 3, 1, 0, 4, 5, 6).reshape(n_dp, n_ctx, *packed.shape)
+
+
+def sum_shards(terms):
+    n_dp, n_ctx = terms.shape[:2]
+    shard = terms.shape[2:]
+    if not own_plan():
+        part = lax.psum_scatter(terms, "dp", scatter_dimension=0)
+        return lax.psum_scatter(part, "ctx", scatter_dimension=0).astype(jnp.float32)
+    sems = pltpu.SemaphoreType.DMA((6, n_ctx))
+    return vmem_call(
+        functools.partial(scatter_kernel, n_ctx),
+        terms.reshape(2, 2, 2, n_ctx, *shard).transpose(3, 2, 0, 1, 4, 5, 6),
+        jax.ShapeDtypeStruct(shard, jnp.float32),
+        [
+            pltpu.VMEM((n_ctx, 2, 2) + shard, terms.dtype),
+            pltpu.VMEM((n_ctx, 2, 2) + shard, terms.dtype),
+            pltpu.VMEM((n_ctx, 2, 2) + shard[1:], terms.dtype),
+            pltpu.VMEM((n_ctx, 2, 2) + shard[1:], terms.dtype),
+            pltpu.VMEM((n_ctx,) + shard, terms.dtype),
+            pltpu.VMEM((n_ctx,) + shard, terms.dtype),
+            pltpu.VMEM((n_ctx,) + shard, terms.dtype),
+            sems,
+            sems,
+        ],
+        4,
+    )
+
+
+GAIN_ROWS = 8
 
 
 def gather_weights(
@@ -67,27 +379,73 @@
     attention_gain,
     feedforward_gain,
 ):
-    wide_mats = (
-        lax.all_gather(query_weight, "ctx", axis=1, tiled=True),
-        lax.all_gather(key_weight, "ctx", axis=1, tiled=True),
-        lax.all_gather(value_weight, "ctx", axis=1, tiled=True),
-        lax.all_gather(output_weight, "ctx", axis=1, tiled=True),
-        lax.all_gather(gate_weight, "ctx", axis=1, tiled=True),
-        lax.all_gather(up_weight, "ctx", axis=1, tiled=True),
-        lax.all_gather(down_weight, "ctx", axis=1, tiled=True),
-    )
-    whole_set = (
-        lax.all_gather(wide_mats[0], "dp", axis=0, tiled=True),
-        lax.all_gather(wide_mats[1], "dp", axis=0, tiled=True),
-        lax.all_gather(wide_mats[2], "dp", axis=0, tiled=True),
-        lax.all_gather(wide_mats[3], "dp", axis=0, tiled=True),
-        lax.all_gather(wide_mats[4], "dp", axis=0, tiled=True),
-        lax.all_gather(wide_mats[5], "dp", axis=0, tiled=True),
-        lax.all_gather(wide_mats[6], "dp", axis=0, tiled=True),
-        lax.all_gather(attention_gain, "dp", axis=0, tiled=True),
-        lax.all_gather(feedforward_gain, "dp", axis=0, tiled=True),
-    )
-    return whole_set
+    n_dp, n_ctx = lax.axis_size("dp"), lax.axis_size("ctx")
+    rows = query_weight.shape[0]
+    width = 2 * gate_weight.shape[1]
+    blocks = down_weight.shape[1] // rows
+    down_side = down_weight.T.reshape(blocks, rows, -1).swapaxes(0, 1).reshape(rows, -1)
+    half_a = jnp.concatenate(
+        [query_weight, key_weight, value_weight, output_weight, gate_weight], axis=1
+    )
+    half_b = jnp.concatenate([up_weight, down_side], axis=1)
+    gains = jnp.stack([attention_gain, feedforward_gain], axis=0)
+    gains = jnp.pad(gains, ((0, GAIN_ROWS - 2), (0, width - rows)))
+    packed = jnp.stack(
+        [jnp.concatenate([half_a, gains], axis=0), jnp.concatenate([half_b, gains], axis=0)]
+    )
+    shards = all_shards(packed)
+
+    def whole(half, start, stop):
+        part = shards[:, :, half, :rows, start:stop]
+        return part.transpose(0, 2, 1, 3).reshape(n_dp * rows, n_ctx * (stop - start))
+
+    mats, start = [], 0
+    for item in (query_weight, key_weight, value_weight, output_weight, gate_weight):
+        mats.append(whole(0, start, start + item.shape[1]))
+        start += item.shape[1]
+    mats.append(whole(1, 0, up_weight.shape[1]))
+    down_part = shards[:, :, 1, :rows, up_weight.shape[1] :]
+    down_part = down_part.reshape(n_dp, n_ctx, rows, blocks, -1).transpose(1, 3, 2, 0, 4)
+    mats.append(down_part.reshape(n_ctx * blocks * rows, -1))
+    gain_part = shards[:, 0, 0, rows : rows + 2, :rows]
+    mats.append(gain_part[:, 0].reshape(-1))
+    mats.append(gain_part[:, 1].reshape(-1))
+    return tuple(mats)
+
+
+def scatter_grads(query, key, value, output, gate, up, down_side, attn_gain, ffn_gain):
+    n_dp, n_ctx = lax.axis_size("dp"), lax.axis_size("ctx")
+    rows = query.shape[0] // n_dp
+    width = 2 * gate.shape[1] // n_ctx
+    blocks = down_side.shape[0] // (n_ctx * rows)
+
+    def parts(item):
+        item = item.astype(jnp.bfloat16)
+        return item.reshape(n_dp, rows, n_ctx, -1).transpose(0, 2, 1, 3)
+
+    down_part = down_side.astype(jnp.bfloat16).reshape(n_ctx, blocks, rows, n_dp, -1)
+    down_part = down_part.transpose(3, 0, 2, 1, 4).reshape(n_dp, n_ctx, rows, -1)
+    half_a = jnp.concatenate([parts(item) for item in (query, key, value, output, gate)], axis=-1)
+    half_b = jnp.concatenate([parts(up), down_part], axis=-1)
+    gains = jnp.stack([attn_gain.reshape(n_dp, rows), ffn_gain.reshape(n_dp, rows)], axis=1)
+    gains = jnp.pad(gains.astype(jnp.bfloat16), ((0, 0), (0, GAIN_ROWS - 2), (0, width - rows)))
+    gains = jnp.broadcast_to(gains[:, None], (n_dp, n_ctx, GAIN_ROWS, width))
+    terms = jnp.stack(
+        [jnp.concatenate([half_a, gains], axis=2), jnp.concatenate([half_b, gains], axis=2)], axis=2
+    )
+    total = sum_shards(terms)
+    grads, start = [], 0
+    for item in (query, key, value, output, gate):
+        stop = start + item.shape[1] // n_ctx
+        grads.append(total[0, :rows, start:stop])
+        start = stop
+    up_stop = up.shape[1] // n_ctx
+    grads.append(total[1, :rows, :up_stop])
+    down_own = total[1, :rows, up_stop:].reshape(rows, blocks, -1).swapaxes(0, 1)
+    grads.append(down_own.reshape(blocks * rows, -1).T)
+    grads.append(total[0, rows, :rows])
+    grads.append(total[0, rows + 1, :rows])
+    return tuple(grads)
 
 
 def masked_scores(query_rot, key_all, query_pos, key_pos):
@@ -135,10 +493,10 @@
         .astype(jnp.bfloat16)
         .reshape(seq_count, span_len, KV_HEADS * HEAD_DIM)
     )
-    key_all, value_all = (
-        lax.all_gather(key_rot, "ctx", axis=1, tiled=True),
-        lax.all_gather(value_low, "ctx", axis=1, tiled=True),
-    )
+    kv_width = KV_HEADS * HEAD_DIM
+    both_all = span_gather(jnp.concatenate([key_rot, value_low], axis=-1))
+    both_all = jnp.swapaxes(both_all, 0, 1).reshape(seq_count, ctx_parts * span_len, 2 * kv_width)
+    key_all, value_all = both_all[..., :kv_width], both_all[..., kv_width:]
     scaled = masked_scores(query_rot, key_all, query_pos, key_pos)
     row_peak = jnp.max(scaled, axis=-1, keepdims=True)
     exponent = jnp.exp(scaled - row_peak)
@@ -159,7 +517,7 @@
     up_act = jnp.dot(hidden, up_mat, preferred_element_type=jnp.float32)
     sigmoid_gate = jax.nn.sigmoid(gate_act)
     inner = (gate_act * sigmoid_gate * up_act).astype(jnp.bfloat16)
-    result = middle + jnp.dot(inner, down_mat, preferred_element_type=jnp.float32)
+    result = middle + transposed_product(inner, down_mat)
     kept_state = (
         inverse_one,
         norm_one,
@@ -214,7 +572,7 @@
     key_length = key_all.shape[1]
     group_size = HEADS // KV_HEADS
     cot_rows = micro_cot.reshape(row_count, model_width)
-    d_inner = transposed_product(cot_rows, down_mat)
+    d_inner = jnp.dot(cot_rows, down_mat, preferred_element_type=jnp.float32)
     silu_slope = sigmoid_gate + gate_act * sigmoid_gate * (1.0 - sigmoid_gate)
     d_gate = (d_inner * up_act * silu_slope).astype(jnp.bfloat16)
     d_up = (d_inner * (gate_act * sigmoid_gate)).astype(jnp.bfloat16)
@@ -250,20 +608,19 @@
     key_term = jnp.einsum(
         "shgqk,sqhgd->skhd", d_scores, query_groups, preferred_element_type=jnp.float32
     )
-    d_key_rot, d_value = (
-        lax.psum_scatter(
-            key_term.reshape(seq_count, key_length, KV_HEADS * HEAD_DIM).astype(jnp.bfloat16),
-            "ctx",
-            scatter_dimension=1,
-            tiled=True,
-        ).astype(jnp.float32),
-        lax.psum_scatter(
-            value_term.reshape(seq_count, key_length, KV_HEADS * HEAD_DIM).astype(jnp.bfloat16),
-            "ctx",
-            scatter_dimension=1,
-            tiled=True,
-        ).astype(jnp.float32),
-    )
+    kv_width = KV_HEADS * HEAD_DIM
+    both_terms = jnp.concatenate(
+        [
+            key_term.reshape(seq_count, key_length, kv_width),
+            value_term.reshape(seq_count, key_length, kv_width),
+        ],
+        axis=-1,
+    ).astype(jnp.bfloat16)
+    both_terms = jnp.swapaxes(
+        both_terms.reshape(seq_count, key_length // span_len, -1, 2 * kv_width), 0, 1
+    )
+    both_sum = span_scatter(both_terms)
+    d_key_rot, d_value = both_sum[..., :kv_width], both_sum[..., kv_width:]
     d_query = (
         unrotate(d_query_rot.reshape(seq_count, span_len, HEADS, HEAD_DIM), cos_table, sin_table)
         .reshape(row_count, HEADS * HEAD_DIM)
@@ -318,121 +675,42 @@
     feedforward_gain,
 ):
     ctx_index = lax.axis_index("ctx")
-    outputs_list = []
-    grads_list = []
-    rows_list = []
-    attn_gain_total = None
-    ffn_gain_total = None
-    for micro_step in range(tokens.shape[0]):
-        whole_set = gather_weights(
-            query_weight,
-            key_weight,
-            value_weight,
-            output_weight,
-            gate_weight,
-            up_weight,
-            down_weight,
-            attention_gain,
-            feedforward_gain,
-        )
-        layer_out, kept_state = forward_pass(
-            tokens[micro_step], span_order[micro_step], whole_set, ctx_index
-        )
-        token_grad, product_rows, attn_gain_grad, ffn_gain_grad = backward_pass(
-            cotangent[micro_step], kept_state, whole_set
-        )
-        outputs_list.append(layer_out)
-        grads_list.append(token_grad)
-        rows_list.append(product_rows)
-        if attn_gain_total is None:
-            attn_gain_total = attn_gain_grad
-            ffn_gain_total = ffn_gain_grad
-        else:
-            attn_gain_total = attn_gain_total + attn_gain_grad
-            ffn_gain_total = ffn_gain_total + ffn_gain_grad
-    joined = [
-        jnp.concatenate([rows_item[index] for rows_item in rows_list], axis=0) for index in range(8)
-    ]
-    query_width = query_weight.shape[1] * lax.axis_size("ctx")
-    kv_width = key_weight.shape[1] * lax.axis_size("ctx")
-    ff_width = gate_weight.shape[1] * lax.axis_size("ctx")
-    attn_in_grad = rows_product(joined[0], joined[1])
-    output_grad = rows_product(joined[2], joined[3])
-    ffn_in_grad = rows_product(joined[4], joined[5])
-    down_grad = rows_product(joined[6], joined[7])
-    query_grad = attn_in_grad[:, :query_width]
-    key_grad = attn_in_grad[:, query_width : query_width + kv_width]
-    value_grad = attn_in_grad[:, query_width + kv_width :]
-    gate_grad = ffn_in_grad[:, :ff_width]
-    up_grad = ffn_in_grad[:, ff_width:]
-    row_parts = (
-        lax.psum_scatter(
-            query_grad.astype(jnp.bfloat16), "dp", scatter_dimension=0, tiled=True
-        ).astype(jnp.float32),
-        lax.psum_scatter(
-            key_grad.astype(jnp.bfloat16), "dp", scatter_dimension=0, tiled=True
-        ).astype(jnp.float32),
-        lax.psum_scatter(
-            value_grad.astype(jnp.bfloat16), "dp", scatter_dimension=0, tiled=True
-        ).astype(jnp.float32),
-        lax.psum_scatter(
-            output_grad.astype(jnp.bfloat16), "dp", scatter_dimension=0, tiled=True
-        ).astype(jnp.float32),
-        lax.psum_scatter(
-            gate_grad.astype(jnp.bfloat16), "dp", scatter_dimension=0, tiled=True
-        ).astype(jnp.float32),
-        lax.psum_scatter(
-            up_grad.astype(jnp.bfloat16), "dp", scatter_dimension=0, tiled=True
-        ).astype(jnp.float32),
-        lax.psum_scatter(
-            down_grad.astype(jnp.bfloat16), "dp", scatter_dimension=0, tiled=True
-        ).astype(jnp.float32),
-        lax.psum_scatter(
-            attn_gain_total.astype(jnp.bfloat16), "dp", scatter_dimension=0, tiled=True
-        ).astype(jnp.float32),
-        lax.psum_scatter(
-            ffn_gain_total.astype(jnp.bfloat16), "dp", scatter_dimension=0, tiled=True
-        ).astype(jnp.float32),
-    )
-    final_mats = (
-        lax.psum_scatter(
-            row_parts[0].astype(jnp.bfloat16), "ctx", scatter_dimension=1, tiled=True
-        ).astype(jnp.float32),
-        lax.psum_scatter(
-            row_parts[1].astype(jnp.bfloat16), "ctx", scatter_dimension=1, tiled=True
-        ).astype(jnp.float32),
-        lax.psum_scatter(
-            row_parts[2].astype(jnp.bfloat16), "ctx", scatter_dimension=1, tiled=True
-        ).astype(jnp.float32),
-        lax.psum_scatter(
-            row_parts[3].astype(jnp.bfloat16), "ctx", scatter_dimension=1, tiled=True
-        ).astype(jnp.float32),
-        lax.psum_scatter(
-            row_parts[4].astype(jnp.bfloat16), "ctx", scatter_dimension=1, tiled=True
-        ).astype(jnp.float32),
-        lax.psum_scatter(
-            row_parts[5].astype(jnp.bfloat16), "ctx", scatter_dimension=1, tiled=True
-        ).astype(jnp.float32),
-        lax.psum_scatter(
-            row_parts[6].astype(jnp.bfloat16), "ctx", scatter_dimension=1, tiled=True
-        ).astype(jnp.float32),
-    )
-    final_gains = lax.psum((row_parts[7], row_parts[8]), "ctx")
-    layer_output = jnp.stack(outputs_list, axis=0)
-    input_grad = jnp.stack(grads_list, axis=0)
-    return (
-        layer_output,
-        input_grad,
-        final_mats[0],
-        final_mats[1],
-        final_mats[2],
-        final_mats[3],
-        final_mats[4],
-        final_mats[5],
-        final_mats[6],
-        final_gains[0],
-        final_gains[1],
-    )
+    whole_set = gather_weights(
+        query_weight,
+        key_weight,
+        value_weight,
+        output_weight,
+        gate_weight,
+        up_weight,
+        down_weight,
+        attention_gain,
+        feedforward_gain,
+    )
+    rows_shape = (-1,) + tokens.shape[2:]
+    layer_out, kept_state = forward_pass(
+        tokens.reshape(rows_shape),
+        span_order.reshape(-1, span_order.shape[-1]),
+        whole_set,
+        ctx_index,
+    )
+    token_grad, product_rows, attn_gain_grad, ffn_gain_grad = backward_pass(
+        cotangent.reshape(rows_shape), kept_state, whole_set
+    )
+    normed, d_heads, mixed, d_branch, hidden, d_wide, inner, cot_rows = product_rows
+    query_width, kv_width = whole_set[0].shape[1], whole_set[1].shape[1]
+    ff_width = whole_set[4].shape[1]
+    grads = scatter_grads(
+        rows_product(normed, d_heads[:, :query_width]),
+        rows_product(normed, d_heads[:, query_width : query_width + kv_width]),
+        rows_product(normed, d_heads[:, query_width + kv_width :]),
+        rows_product(mixed, d_branch),
+        rows_product(hidden, d_wide[:, :ff_width]),
+        rows_product(hidden, d_wide[:, ff_width:]),
+        rows_product(cot_rows, inner),
+        attn_gain_grad,
+        ffn_gain_grad,
+    )
+    return (layer_out.reshape(tokens.shape), token_grad.reshape(tokens.shape)) + grads
 
 
 def solution(mesh):

time: 822 us -> 487 us (0.59)
  waiting for transfers between devices: 374 us -> 0 us
  blocking collectives: 234 us -> 0 us
  Pallas kernels: 0 us -> 183 us
  local copies, waits for them, and re-layouts: 38.4 us -> 142 us
  matrix products: 98.4 us -> 129 us
  other arithmetic: 49.6 us -> 25.8 us
  between operations: 17.4 us -> 2.14 us
    reduce_scatter x9 -> x0, waiting for transfers between devices: 210 us -> none  [the longest x1 40.8 us: per_device(): lax.psum_scatter(up_grad.astype(jnp.bfloat16), 'dp', scatter_dimension=0,...]
    all_gather x15 -> x0, blocking collectives: 197 us -> none  [the longest x2 29.8 us: forward_pass(): lax.all_gather(key_rot, 'ctx', axis=1, tiled=True)]
    pallas_call x0 -> x4, Pallas kernels: none -> 183 us  [vmem_call(): pl.pallas_call(kernel, out_shape=out_shape, in_specs=[whole], out_specs=w...]
    unnamed x30 -> x0, waiting for transfers between devices: 164 us -> none
    reshape x0 -> x21, local copies, waits for them, and re-layouts: none -> 39.3 us  [the longest x10 15.1 us: parts(): return item.reshape(n_dp, rows, n_ctx, -1).transpose(0, 2, 1, 3)]
    another operation x14 -> x8, other arithmetic: 29.6 us -> 3.59 us
    unnamed x2 -> x0, blocking collectives: 24.7 us -> none
    transpose x0 -> x12, local copies, waits for them, and re-layouts: none -> 23.8 us  [the longest x8 12.1 us: whole(): part.transpose(0, 2, 1, 3).reshape(n_dp * rows, n_ctx * (stop - start))]
  transfers between devices with their start and end apart: 21 -> 0, of which waited for: 16 -> 0; matrix products, arithmetic and copies ran while one was open for 18% -> 0% of each run, Pallas kernels for 0% -> 0%
where the time goes in v1:
time: 487 us; the launch traced here: 482 us
  Pallas kernels  183 us (38%)
  local copies, waits for them, and re-layouts  142 us (29%)
  matrix products  129 us (26%)
  other arithmetic  25.8 us (5%)
    pallas_call x4, Pallas kernels, vmem_call(): pl.pallas_call(kernel, out_shape=out_shape, in_specs=[whole], out_specs=w...  183 us
    dot_general x1, matrix products, backward_pass(): jnp.einsum('shgqk,sqhgd->skhd', d_scores, query_groups, preferred_element...  26.7 us
    dot_general x1, matrix products, backward_pass(): jnp.einsum('shgqk,skhd->sqhgd', d_scores, key_heads, preferred_element_ty...  26.5 us
    unnamed x110, local copies, waits for them, and re-layouts  16.8 us
    reshape x10, local copies, waits for them, and re-layouts, parts(): return item.reshape(n_dp, rows, n_ctx, -1).transpose(0, 2, 1, 3)  15.1 us
    dot_general x7, matrix products, rows_product(): lax.dot_general(left_mat, right_mat, (((0,), (0,)), ((), ())), preferred_...  13.2 us
    transpose x8, local copies, waits for them, and re-layouts, whole(): part.transpose(0, 2, 1, 3).reshape(n_dp * rows, n_ctx * (stop - start))  12.1 us
    another operation x2, local copies, waits for them, and re-layouts, gather_weights(): down_part.reshape(n_dp, n_ctx, rows, blocks, -1).transpose(1, 3, 2, 0, 4)  11.4 us

profile of v1, /device:TPU:0, one launch (start us, length us, event | category | flops | bytes accessed | tf_op | source)
XLA Modules:
  0.0 481.9 jit_solution(366366908087432016)
XLA Ops:
  4.3 47.4 %shard_map.203 = bf16[4,2,2,2,2,80,768]{6,5,4,3,2,1,0:T(8,128)(2,1)} custom-call(bf16[2,80,768]{2,1,0:T(8,128)(2,1)} %pad_maximum_fusion.9.own_ref), custom_call_target="tpu_custom_call" | custom-call | tf_op jit(solution)/shard_map/pallas_call | solution.py:280
  51.7 3.7 copy.144
  55.4 3.2 copy-done
  58.6 2.0 slice_bitcast_fusion.2
  60.6 2.0 copy.157
  64.5 2.6 slice_bitcast_fusion.5
  75.5 39.0 %shard_map.204 = bf16[4,512,384]{2,1,0:T(8,128)(2,1)} custom-call(bf16[512,384]{1,0:T(8,128)(2,1)} %pad_maximum_fusion.6.own_ref), custom_call_target="tpu_custom_call" | custom-call | tf_op jit(solution)/shard_map/pallas_call | solution.py:280
  117.9 2.2 copy.152
  120.1 2.2 copy.153
  122.3 2.6 copy.154
  124.9 2.1 reshape.424
  129.1 8.2 %fusion.54 = (f32[2,3,3,256]{3,2,1,0:T(4,128)S(1)}, f32[2,3,3,256,1024]{3,4,2,1,0:T(8,128)}) fusion(bf16[2,1024,3,64,1]{1,3,4,2,0:T(8,128)(2,1)S(1)} %bitcast.332, bf16[2,256,3,3,32]{1,4,3,2,0:T(8,128)(2,1)S(1)} %bitcast.361, bf16[2,256,3,3,32]{1,4,3,2,0:T(8,128)(2,1)S(1)} %bitcast.359, pred[2,256,1024]{1,2,0:T(8,128)(4,1)S(1)} %broadcast_compare_fusion), kind=kOutput, calls=%fused_computation.149 | convolution fusion | flops 619310592 | bytes 20793344 | tf_op jit(solution)/shard_map/sqhgd,skhd->shgqk/dot_general | solution.py:456
  137.4 9.0 %fusion.4 = f32[2,3,3,256]{3,2,1,0:T(4,128)S(1)} fusion(f32[2,3,3,256,1024]{3,4,2,1,0:T(8,128)} %get-tuple-element.101, f32[2,3,3,256]{3,2,1,0:T(4,128)S(1)} %get-tuple-element.100), kind=kLoop, calls=%fused_computation.10 | loop fusion | flops 9432576 | bytes 18911232 | tf_op jit(solution)/shard_map/reduce_sum | solution.py:503
  146.4 8.2 %fusion.23 = bf16[2,256,3,3,64]{1,4,3,2,0:T(8,128)(2,1)S(1)} fusion(bf16[2,1024,3,64,1]{1,3,4,2,0:T(8,128)(2,1)S(1)} %bitcast.334, f32[2,3,3,256,1024]{3,4,2,1,0:T(8,128)} %get-tuple-element.101, f32[2,3,3,256]{3,2,1,0:T(4,128)S(1)} %fusion.4, f32[2,3,3,256]{3,2,1,0:T(4,128)S(1)} %get-tuple-element.100), kind=kOutput, calls=%fused_computation.52 | convolution fusion | flops 618430464 | bytes 20287488 | tf_op jit(solution)/shard_map/shgqk,skhd->sqhgd/dot_general | solution.py:508
  156.6 4.9 %fusion.51 = (bf16[8,4,1,72,384]{4,3,2,1,0:T(8,128)(2,1)}, bf16[8,72,4,384]{3,1,2,0:T(8,128)(2,1)S(1)}, bf16[8,72,4,384]{3,1,2,0:T(8,128)(2,1)S(1)}) fusion(bf16[8,4,2,80,768]{4,3,2,1,0:T(8,128)(2,1)} %bitcast.307), kind=kLoop, calls=%fused_computation.146 | loop fusion | bytes 10616832 | tf_op jit(solution)/shard_map/slice | solution.py:407
  162.5 3.1 fusion.55
  166.6 3.1 fusion.56
  169.7 6.9 %reshape_squeeze.8 = bf16[8,4,72,2,192]{4,3,2,1,0:T(2,128)(2,1)} reshape(bf16[8,4,1,72,384]{4,3,2,1,0:T(8,128)(2,1)} %get-tuple-element.61) | data formatting | bytes 3538944 | tf_op jit(solution)/shard_map/reshape;squeeze | solution.py:408
  176.7 4.5 copy.223
  181.1 4.7 reshape.428
  187.7 5.9 %multiply_convert_fusion = (bf16[512,1536]{1,0:T(8,128)(2,1)}, bf16[512,1536]{1,0:T(8,128)(2,1)}, bf16[512,1536]{1,0:T(8,128)(2,1)S(1)}) fusion(f32[512,1536]{1,0:T(8,128)} %fusion.55, f32[512,1536]{1,0:T(8,128)} %fusion.56, bf16[576,1536]{1,0:T(8,128)(2,1)S(1)} %copy-done.23, bf16[512,576]{0,1:T(8,128)(2,1)S(1)} %bitcast.347), kind=kOutput, calls=%fused_computation.23 | convolution fusion | flops 916979712 | bytes 13369344 | tf_op jit(solution)/shard_map/dot_general | solution.py:575
  196.7 2.6 reshape_reshape.9
  201.3 3.2 fusion.57
  209.7 2.8 reshape.429
  212.5 10.4 %fusion.29 = f32[2,3,1024,256,3]{3,2,4,1,0:T(8,128)} fusion(bf16[2,1024,3,64,1]{1,3,4,2,0:T(8,128)(2,1)} %bitcast.333, bf16[2,256,3,3,64]{1,0,4,3,2:T(2,128)(2,1)} %reshape.429), kind=kOutput, calls=%fused_computation.85 | convolution fusion | flops 603979776 | bytes 20250624 | tf_op jit(solution)/shard_map/sqhgd,skhd->shgqk/dot_general | solution.py:597
  222.9 26.5 %fusion.12 = f32[2,3,64,3,256]{4,2,3,1,0:T(8,128)} fusion(bf16[2,1024,3,64,1]{1,3,4,2,0:T(8,128)(2,1)} %bitcast.331, f32[2,3,1024,256,3]{3,2,4,1,0:T(8,128)} %fusion.29, f32[2,3,3,256,1024]{3,4,2,1,0:T(8,128)} %get-tuple-element.101, f32[2,3,3,256]{3,2,1,0:T(4,128)S(1)} %log_add_fusion), kind=kOutput, calls=%fused_computation.19 | convolution fusion | flops 637015552 | bytes 39733248 | tf_op jit(solution)/shard_map/shgqk,skhd->sqhgd/dot_general | solution.py:605
  254.2 10.3 %fusion.20 = bf16[2,1024,3,64]{1,3,2,0:T(8,128)(2,1)} fusion(f32[2,3,3,256,1024]{3,4,2,1,0:T(8,128)} %get-tuple-element.101, f32[2,3,3,256]{3,2,1,0:T(4,128)S(1)} %log_add_fusion, bf16[2,256,3,3,64]{1,0,4,3,2:T(2,128)(2,1)S(1)} %copy-done.7), kind=kOutput, calls=%fused_computation.51 | convolution fusion | flops 613810176 | bytes 20269056 | tf_op jit(solution)/shard_map/shgqk,sqhgd->skhd/dot_general | solution.py:600
  264.5 2.6 concatenate.70
  267.1 2.3 copy.170
  269.5 26.7 %fusion.19 = bf16[2,1024,3,64]{1,3,2,0:T(8,128)(2,1)} fusion(f32[2,3,1024,256,3]{3,2,4,1,0:T(8,128)} %fusion.29, f32[2,3,3,256,1024]{3,4,2,1,0:T(8,128)} %get-tuple-element.101, f32[2,3,3,256]{3,2,1,0:T(4,128)S(1)} %log_add_fusion, bf16[2,256,3,3,32]{1,4,3,2,0:T(8,128)(2,1)} %bitcast.362, bf16[2,256,3,3,32]{1,4,3,2,0:T(8,128)(2,1)} %bitcast.360), kind=kOutput, calls=%fused_computation.50 | convolution fusion | flops 638588416 | bytes 39143424 | tf_op jit(solution)/shard_map/shgqk,sqhgd->skhd/dot_general | solution.py:608
  296.2 2.6 concatenate.69
  298.8 2.3 copy.169
  301.1 3.3 pad_maximum_fusion.3
  304.4 39.4 %shard_map.205 = f32[512,384]{1,0:T(8,128)} custom-call(bf16[4,512,384]{2,1,0:T(8,128)(2,1)} %bitcast.326), custom_call_target="tpu_custom_call" | custom-call | tf_op jit(solution)/shard_map/pallas_call | solution.py:280
  345.8 2.0 copy.171
  352.8 2.9 reshape_reshape.11
  355.7 2.4 copy.185
  362.4 3.3 reshape.434
  371.5 2.5 convolution_convert_fusion.2
  375.9 6.5 %concatenate.73 = bf16[8,4,72,768]{3,2,1,0:T(8,128)(2,1)S(1)} concatenate(bf16[8,4,72,144]{3,2,1,0:T(8,128)(2,1)} %get-tuple-element.107, bf16[8,4,72,48]{3,2,1,0:T(8,128)(2,1)} %bitcast.337, bf16[8,4,72,48]{3,2,1,0:T(8,128)(2,1)} %bitcast.338, bf16[8,4,72,144]{3,2,1,0:T(8,128)(2,1)} %get-tuple-element.106, bf16[8,4,72,384]{3,2,1,0:T(8,128)(2,1)} %bitcast.325), dimensions={3} | concatenate | bytes 7077888 | tf_op jit(solution)/shard_map/concatenate | solution.py:428
  382.4 3.9 fusion.13
  386.3 4.6 reshape.440
  390.9 5.5 %copy.180 = bf16[8,4,72,2,192]{4,3,2,1,0:T(2,128)(2,1)} copy(bf16[8,4,72,2,192]{4,0,2,3,1:T(8,128)(2,1)} %bitcast.315) | data formatting | bytes 3538944 | tf_op jit(solution)/shard_map/transpose | solution.py:427
  396.4 6.0 %reshape.441 = bf16[8,4,72,384]{3,2,1,0:T(8,128)(2,1)} reshape(bf16[8,4,72,2,192]{4,3,2,1,0:T(2,128)(2,1)} %copy.180) | data formatting | bytes 3538944 | tf_op jit(solution)/shard_map/reshape | solution.py:427
  402.4 3.9 convolution_convert_fusion.1
  406.2 4.1 reshape.439
  413.2 3.5 copy_bitcast_fusion.term_ref
  416.7 57.0 %shard_map.206 = f32[2,80,768]{2,1,0:T(8,128)} custom-call(bf16[4,2,2,2,2,80,768]{6,5,4,3,2,1,0:T(8,128)(2,1)} %copy_bitcast_fusion.term_ref), custom_call_target="tpu_custom_call" | custom-call | tf_op jit(solution)/shard_map/pallas_call | solution.py:280
  (197 shorter events, 69.0 us)
Async XLA Ops:
  0.6 1.9 copy-start.40
  0.7 1.9 copy-start.41
  0.7 2.1 copy-start.34
  0.7 1.9 copy-start.36
  0.7 2.0 copy-start.37
  0.7 2.1 copy-start.35
  0.7 2.1 copy-start.32
  2.4 0.9 copy-start.31
  2.5 1.0 copy-start.33
  55.4 3.2 copy-start
  64.5 4.0 copy-start.10
  67.6 1.9 copy-start.18
  69.9 2.1 copy-start.38
  127.0 0.9 copy-start.2
  127.9 1.2 copy-start.12
  128.1 9.3 %copy-start.27 = (bf16[2,256,9,32]{1,3,2,0:T(8,128)(2,1)}, bf16[2,256,9,32]{1,3,2,0:T(8,128)(2,1)S(1)}, u32[]{:S(2)}) copy-start(bf16[2,256,9,32]{1,3,2,0:T(8,128)(2,1)S(1)} %get-tuple-element.75) | copy-start | bytes 884740
  128.1 9.3 %copy-start.28 = (bf16[2,256,9,32]{1,3,2,0:T(8,128)(2,1)}, bf16[2,256,9,32]{1,3,2,0:T(8,128)(2,1)S(1)}, u32[]{:S(2)}) copy-start(bf16[2,256,9,32]{1,3,2,0:T(8,128)(2,1)S(1)} %get-tuple-element.76) | copy-start | bytes 884740
  137.4 9.0 %copy-start.13 = (bf16[2,1024,192]{1,2,0:T(8,128)(2,1)S(1)}, bf16[2,1024,192]{1,2,0:T(8,128)(2,1)}, u32[]{:S(2)}) copy-start(bf16[2,1024,192]{1,2,0:T(8,128)(2,1)} %copy.152) | copy-start | bytes 2359300
  154.6 1.1 copy-start.5
  155.3 1.0 copy-start.8
  156.3 48.2 %copy-start.1 = (f32[512,576]{0,1:T(8,128)}, f32[512,576]{0,1:T(8,128)S(1)}, u32[]{:S(2)}) copy-start(f32[512,576]{0,1:T(8,128)S(1)} %get-tuple-element.103) | copy-start | bytes 3538948
  156.6 10.0 %copy-start.29 = (bf16[512,576]{0,1:T(8,128)(2,1)}, bf16[512,576]{0,1:T(8,128)(2,1)S(1)}, u32[]{:S(2)}) copy-start(bf16[512,576]{0,1:T(8,128)(2,1)S(1)} %multiply_convert_fusion.3) | copy-start | bytes 1769476
  162.4 3.1 copy-start.22
  166.6 3.2 copy-start.20
  185.8 1.9 copy-start.23
  187.7 5.9 %copy-start.16 = (bf16[72,8,2,256]{3,1,2,0:T(8,128)(2,1)}, bf16[72,8,2,256]{3,1,2,0:T(8,128)(2,1)S(1)}, u32[]{:S(2)}) copy-start(bf16[72,8,2,256]{3,1,2,0:T(8,128)(2,1)S(1)} %copy.208) | copy-start | bytes 1769476
  193.7 1.1 copy-start.43
  201.3 3.2 copy-start.21
  201.3 3.2 copy-start.42
  204.6 1.9 copy-start.17
  206.5 1.7 copy-start.6
  250.9 1.6 copy-start.3
  251.6 2.6 copy-start.7
  251.7 0.8 copy-start.14
  347.8 1.5 copy-start.11
  349.2 1.6 copy-start.19
  349.2 1.6 copy-start.24
  355.7 2.4 copy-start.39
  355.7 3.4 copy-start.9
  359.8 1.1 copy-start.15
  365.8 1.8 copy-start.25
  368.3 3.1 copy-start.30
  410.3 2.0 copy-start.4
  410.3 2.1 copy-start.26
